TPU v7x, 512 devices: a whole 4x8x8 slice. The times are simulated.
512 devices in a mesh: loop: 16 (over z_hi, x, core), grp: 32 (over y, z_lo).
Axes of the slice: x: 4, y: 8, z: 8 (z_hi: 2, z_lo: 4; z = z_hi * 4 + z_lo), core: 2. Of those that a mesh axis runs over, the one named last changes fastest.
Arguments:
- points: bfloat16 [64, 98304], P(None, ('loop', 'grp')), may hold values from -2 to 2, as said below
- probes: bfloat16 [16, 98304], P(None, ('loop', 'grp')), may hold values from -6 to 6
Outputs:
- product: float32 [16, 98304], P(None, ('loop', 'grp'))
Inputs may be any that keep to these rules, and one draw needn't show every extreme that they name: points drawn around a set of cluster centres with spreads that differ from point to point.
All inputs are finite; a program needn't handle non-finite values.
Results may differ from a plain program's by a relative error of at most 0.0038.
Values may be sent and summed in bfloat16 or wider, within the bound.
A program may use at most 64 MiB of HBM per device.

v0:
```python
import math

import jax
import jax.numpy as jnp
from jax import lax
from jax.sharding import PartitionSpec as P


def shifted(block, axis, distance):
    devices = range(lax.axis_size(axis))
    route = [((i - distance) % len(devices), i) for i in devices]
    return lax.ppermute(block, axis, route)


def norms(block):
    wide = block.astype(jnp.float32)
    return jnp.sum(wide * wide, axis=0)


def matern(xa, na, xb, nb):
    cross = lax.dot_general(xa, xb, (((0,), (0,)), ((), ())), preferred_element_type=jnp.float32)
    dist = jnp.maximum(na[:, None] + nb[None, :] - 2.0 * cross, 0.0)
    scaled = jnp.sqrt(5.0 * dist)
    return ((1.0 + scaled + scaled * scaled / 3.0) * jnp.exp(-scaled)).astype(jnp.bfloat16)


def visit(own_x, own_v, own_n, far_x, far_v, own_y, mirror):
    total = far_x.shape[1]
    width = math.gcd(total, 2048)
    count = total // width
    far_n = norms(far_x)
    start_part = jnp.zeros((own_v.shape[0], total), jnp.float32)

    def advance(index, carry):
        acc_y, part = carry
        start = index * width
        piece_x = lax.dynamic_slice_in_dim(far_x, start, width, 1)
        piece_v = lax.dynamic_slice_in_dim(far_v, start, width, 1)
        piece_n = lax.dynamic_slice_in_dim(far_n, start, width, 0)
        kern = matern(own_x, own_n, piece_x, piece_n)
        acc_y = acc_y + lax.dot_general(
            piece_v, kern, (((1,), (1,)), ((), ())), preferred_element_type=jnp.float32
        )
        if mirror:
            term = jnp.dot(own_v, kern, preferred_element_type=jnp.float32)
            part = lax.dynamic_update_slice_in_dim(part, term, start, 1)
        return (acc_y, part)

    return lax.fori_loop(0, count, advance, (own_y, start_part))


def on_device(points, probes):
    loop_n = lax.axis_size("loop")
    half = loop_n // 2
    total_points = points.shape[1] * loop_n * lax.axis_size("grp")
    own_n = norms(points)
    block_x, block_v = (
        lax.all_gather(points, "grp", axis=1, tiled=True),
        lax.all_gather(probes, "grp", axis=1, tiled=True),
    )
    own_y = jnp.zeros((probes.shape[0], points.shape[1]), jnp.float32)
    own_y, unused = visit(points, probes, own_n, block_x, block_v, own_y, False)
    carried = None
    for step in range(1, half + 1):
        block_x, block_v = shifted((block_x, block_v), "loop", 1)
        mirror = step < half
        own_y, part = visit(points, probes, own_n, block_x, block_v, own_y, mirror)
        if mirror:
            if step == 1:
                carried = part
            else:
                carried = shifted(carried, "loop", 1) + part
    returned = shifted(carried, "loop", 1 - half)
    home = lax.psum_scatter(returned, "grp", scatter_dimension=1, tiled=True)
    return (own_y + home) * float(total_points) ** (-0.5)


def solution(mesh):
    in_specs = (P(None, ("loop", "grp")), P(None, ("loop", "grp")))
    out_specs = P(None, ("loop", "grp"))
    return jax.shard_map(
        on_device, mesh=mesh, in_specs=in_specs, out_specs=out_specs, check_vma=False
    )
```

profile of v0, /device:TPU:4, one launch (start us, length us, event | category | flops | bytes accessed | tf_op | source)
XLA Modules:
  0.0 632.4 jit_solution(6115258733443320652)
XLA Ops:
  6.5 83.3 %all-gather = bf16[32,192,16]{1,2,0:T(8,128)(2,1)S(1)} all-gather(bf16[1,192,16]{1,2,0:T(8,128)(2,1)} %bitcast.282), channel_id=1, replica_groups=mesh['loop'=16,'grp'=32] {'grp'}, dimensions={0}, use_global_device_ids=true | all-gather | bytes 202752 | tf_op jit(solution)/shard_map/all_gather | solution.py:59
  106.0 79.9 %all-gather.1 = bf16[32,192,64]{1,2,0:T(8,128)(2,1)S(1)} all-gather(bf16[1,192,64]{1,2,0:T(8,128)(2,1)} %bitcast.285), channel_id=1, replica_groups=mesh['loop'=16,'grp'=32] {'grp'}, dimensions={0}, use_global_device_ids=true | all-gather | bytes 811008 | tf_op jit(solution)/shard_map/all_gather | solution.py:58
  190.5 13.8 %collective-permute-start.6 = (bf16[16,6144]{1,0:T(8,128)(2,1)S(1)}, bf16[16,6144]{1,0:T(8,128)(2,1)S(1)}, u32[]{:S(2)}, u32[]{:S(2)}) collective-permute-start(bf16[16,6144]{1,0:T(8,128)(2,1)S(1)} %collective-permute-done.4), channel_id=1, source_target_pairs={{480,0},{0,32},{32,64},{64,96},{96,128},{128,160},{160,192},{192,2... | collective-permute-start | bytes 589832 | tf_op jit(solution)/shard_map/ppermute | solution.py:12
  205.6 9.8 %collective-permute-start.8 = (bf16[16,6144]{1,0:T(8,128)(2,1)S(1)}, bf16[16,6144]{1,0:T(8,128)(2,1)S(1)}, u32[]{:S(2)}, u32[]{:S(2)}) collective-permute-start(bf16[16,6144]{1,0:T(8,128)(2,1)S(1)} %collective-permute-done.6), channel_id=1, source_target_pairs={{480,0},{0,32},{32,64},{64,96},{96,128},{128,160},{160,192},{192,2... | collective-permute-start | bytes 589832 | tf_op jit(solution)/shard_map/ppermute | solution.py:12
  228.0 15.6 %collective-permute-start.10 = (bf16[16,6144]{1,0:T(8,128)(2,1)S(1)}, bf16[16,6144]{1,0:T(8,128)(2,1)}, u32[]{:S(2)}, u32[]{:S(2)}) collective-permute-start(bf16[16,6144]{1,0:T(8,128)(2,1)S(1)} %collective-permute-done.8), channel_id=1, source_target_pairs={{480,0},{0,32},{32,64},{64,96},{96,128},{128,160},{160,192},{192,2... | collective-permute-start | bytes 589832 | tf_op jit(solution)/shard_map/ppermute | solution.py:12
  243.6 8.2 %while.132 = (s32[]{:T(128)}, f32[16,192]{1,0:T(8,128)S(1)}, f32[16,6144]{1,0:T(8,128)S(1)}, bf16[16,6144]{1,0:T(8,128)(2,1)S(1)}, f32[192]{0:T(256)S(1)}, /*ind...) while((s32[]{:T(128)}, f32[16,192]{1,0:T(8,128)S(1)}, ...), condition=%wide.region_6.0_spmd, body=%wide.region_5.0_spmd.sunk | while | flops 80219136 | bytes 2905019 | solution.py:49
  251.8 10.5 %collective-permute-start.16 = (f32[16,6144]{1,0:T(8,128)S(1)}, f32[16,6144]{1,0:T(8,128)S(1)}, u32[]{:S(2)}, u32[]{:S(2)}) collective-permute-start(f32[16,6144]{1,0:T(8,128)S(1)} %get-tuple-element.1347), channel_id=1, source_target_pairs={{480,0},{0,32},{32,64},{64,96},{96,128},{128,160},{160,192},{192,2... | collective-permute-start | bytes 1179656 | tf_op jit(solution)/shard_map/ppermute | solution.py:12
  267.1 10.4 %collective-permute-start.5 = (bf16[64,6144]{1,0:T(8,128)(2,1)}, bf16[64,6144]{1,0:T(8,128)(2,1)}, u32[]{:S(2)}, u32[]{:S(2)}) collective-permute-start(bf16[64,6144]{1,0:T(8,128)(2,1)} %collective-permute-done.3), channel_id=1, source_target_pairs={{480,0},{0,32},{32,64},{64,96},{96,128},{128,160},{160,192},{192,2... | collective-permute-start | bytes 2359304 | tf_op jit(solution)/shard_map/ppermute | solution.py:12
  277.5 8.2 %while.133 = (s32[]{:T(128)}, f32[16,192]{1,0:T(8,128)S(1)}, f32[16,6144]{1,0:T(8,128)S(1)}, bf16[16,6144]{1,0:T(8,128)(2,1)S(1)}, f32[192]{0:T(256)S(1)}, /*ind...) while((s32[]{:T(128)}, f32[16,192]{1,0:T(8,128)S(1)}, ...), condition=%wide.region_9.0_spmd, body=%wide.region_8.0_spmd.sunk | while | flops 80219136 | bytes 2905019 | solution.py:49
  285.8 13.1 %collective-permute-start.17 = (f32[16,6144]{1,0:T(8,128)S(1)}, f32[16,6144]{1,0:T(8,128)S(1)}, u32[]{:S(2)}, u32[]{:S(2)}) collective-permute-start(f32[16,6144]{1,0:T(8,128)S(1)} %add.741), channel_id=1, source_target_pairs={{480,0},{0,32},{32,64},{64,96},{96,128},{128,160},{160,192},{192,2... | collective-permute-start | bytes 1179656 | tf_op jit(solution)/shard_map/ppermute | solution.py:12
  300.2 10.5 %collective-permute-start.7 = (bf16[64,6144]{1,0:T(8,128)(2,1)}, bf16[64,6144]{1,0:T(8,128)(2,1)}, u32[]{:S(2)}, u32[]{:S(2)}) collective-permute-start(bf16[64,6144]{1,0:T(8,128)(2,1)} %collective-permute-done.5), channel_id=1, source_target_pairs={{480,0},{0,32},{32,64},{64,96},{96,128},{128,160},{160,192},{192,2... | collective-permute-start | bytes 2359304 | tf_op jit(solution)/shard_map/ppermute | solution.py:12
  310.8 8.2 %while.134 = (s32[]{:T(128)}, f32[16,192]{1,0:T(8,128)S(1)}, f32[16,6144]{1,0:T(8,128)S(1)}, bf16[16,6144]{1,0:T(8,128)(2,1)S(1)}, f32[192]{0:T(256)S(1)}, /*ind...) while((s32[]{:T(128)}, f32[16,192]{1,0:T(8,128)S(1)}, ...), condition=%wide.region_12.0_spmd, body=%wide.region_11.0_spmd.sunk | while | flops 80219136 | bytes 2905019 | solution.py:49
  322.3 9.6 %collective-permute-start.9 = (bf16[64,6144]{1,0:T(8,128)(2,1)}, bf16[64,6144]{1,0:T(8,128)(2,1)}, u32[]{:S(2)}, u32[]{:S(2)}) collective-permute-start(bf16[64,6144]{1,0:T(8,128)(2,1)} %collective-permute-done.7), channel_id=1, source_target_pairs={{480,0},{0,32},{32,64},{64,96},{96,128},{128,160},{160,192},{192,2... | collective-permute-start | bytes 2359304 | tf_op jit(solution)/shard_map/ppermute | solution.py:12
  332.0 8.2 %while.135 = (s32[]{:T(128)}, f32[16,192]{1,0:T(8,128)S(1)}, f32[16,6144]{1,0:T(8,128)S(1)}, bf16[16,6144]{1,0:T(8,128)(2,1)S(1)}, f32[192]{0:T(256)S(1)}, /*ind...) while((s32[]{:T(128)}, f32[16,192]{1,0:T(8,128)S(1)}, ...), condition=%wide.region_15.0_spmd, body=%wide.region_14.0_spmd.sunk | while | flops 80219136 | bytes 2905019 | solution.py:49
  340.2 10.8 %collective-permute-start.19 = (f32[16,6144]{1,0:T(8,128)S(1)}, f32[16,6144]{1,0:T(8,128)S(1)}, u32[]{:S(2)}, u32[]{:S(2)}) collective-permute-start(f32[16,6144]{1,0:T(8,128)S(1)} %add.743), channel_id=1, source_target_pairs={{480,0},{0,32},{32,64},{64,96},{96,128},{128,160},{160,192},{192,2... | collective-permute-start | bytes 1179656 | tf_op jit(solution)/shard_map/ppermute | solution.py:12
  358.6 8.2 %while.136 = (s32[]{:T(128)}, f32[16,192]{1,0:T(8,128)S(1)}, f32[16,6144]{1,0:T(8,128)S(1)}, bf16[16,6144]{1,0:T(8,128)(2,1)S(1)}, f32[192]{0:T(256)S(1)}, /*ind...) while((s32[]{:T(128)}, f32[16,192]{1,0:T(8,128)S(1)}, ...), condition=%wide.region_18.0_spmd, body=%wide.region_17.0_spmd.sunk | while | flops 80219136 | bytes 2905019 | solution.py:49
  366.8 10.5 %collective-permute-start.20 = (f32[16,6144]{1,0:T(8,128)S(1)}, f32[16,6144]{1,0:T(8,128)S(1)}, u32[]{:S(2)}, u32[]{:S(2)}) collective-permute-start(f32[16,6144]{1,0:T(8,128)S(1)} %add.744), channel_id=1, source_target_pairs={{480,0},{0,32},{32,64},{64,96},{96,128},{128,160},{160,192},{192,2... | collective-permute-start | bytes 1179656 | tf_op jit(solution)/shard_map/ppermute | solution.py:12
  378.7 7.4 %collective-permute-start.13 = (bf16[64,6144]{1,0:T(8,128)(2,1)}, bf16[64,6144]{1,0:T(8,128)(2,1)}, u32[]{:S(2)}, u32[]{:S(2)}) collective-permute-start(bf16[64,6144]{1,0:T(8,128)(2,1)} %collective-permute-done.11), channel_id=1, source_target_pairs={{480,0},{0,32},{32,64},{64,96},{96,128},{128,160},{160,192},{192,2... | collective-permute-start | bytes 2359304 | tf_op jit(solution)/shard_map/ppermute | solution.py:12
  386.1 10.7 %while.137 = (s32[]{:T(128)}, f32[16,192]{1,0:T(8,128)S(1)}, f32[16,6144]{1,0:T(8,128)S(1)}, bf16[16,6144]{1,0:T(8,128)(2,1)}, f32[192]{0:T(256)S(1)}, /*index=5...) while((s32[]{:T(128)}, f32[16,192]{1,0:T(8,128)S(1)}, ...), condition=%wide.region_21.0_spmd, body=%wide.region_20.0_spmd.sunk | while | flops 80219136 | bytes 2900923 | solution.py:49
  396.9 10.5 %collective-permute-start.21 = (f32[16,6144]{1,0:T(8,128)S(1)}, f32[16,6144]{1,0:T(8,128)S(1)}, u32[]{:S(2)}, u32[]{:S(2)}) collective-permute-start(f32[16,6144]{1,0:T(8,128)S(1)} %add.745), channel_id=1, source_target_pairs={{480,0},{0,32},{32,64},{64,96},{96,128},{128,160},{160,192},{192,2... | collective-permute-start | bytes 1179656 | tf_op jit(solution)/shard_map/ppermute | solution.py:12
  407.4 7.6 %collective-permute-start.15 = (bf16[64,6144]{1,0:T(8,128)(2,1)}, bf16[64,6144]{1,0:T(8,128)(2,1)S(1)}, u32[]{:S(2)}, u32[]{:S(2)}) collective-permute-start(bf16[64,6144]{1,0:T(8,128)(2,1)} %collective-permute-done.13), channel_id=1, source_target_pairs={{480,0},{0,32},{32,64},{64,96},{96,128},{128,160},{160,192},{192,2... | collective-permute-start | bytes 2359304 | tf_op jit(solution)/shard_map/ppermute | solution.py:12
  416.4 8.2 %while.138 = (s32[]{:T(128)}, f32[16,192]{1,0:T(8,128)S(1)}, f32[16,6144]{1,0:T(8,128)S(1)}, bf16[16,6144]{1,0:T(8,128)(2,1)S(1)}, f32[192]{0:T(256)S(1)}, /*ind...) while((s32[]{:T(128)}, f32[16,192]{1,0:T(8,128)S(1)}, ...), condition=%wide.region_24.0_spmd, body=%wide.region_23.0_spmd.sunk | while | flops 80219136 | bytes 2905019 | solution.py:49
  424.7 13.1 %collective-permute-start.22 = (f32[16,6144]{1,0:T(8,128)S(1)}, f32[16,6144]{1,0:T(8,128)S(1)}, u32[]{:S(2)}, u32[]{:S(2)}) collective-permute-start(f32[16,6144]{1,0:T(8,128)S(1)} %add.746), channel_id=1, source_target_pairs={{224,0},{256,32},{288,64},{320,96},{352,128},{384,160},{416,192},{... | collective-permute-start | bytes 1179656 | tf_op jit(solution)/shard_map/ppermute | solution.py:12
  451.0 173.0 %reduce-scatter.4.cloned.1.call-done = f32[192,16]{1,0:T(8,128)} async-done(((f32[6144,16]{1,0:T(8,128)}), f32[192,16]{1,0:T(8,128)}) %reduce-scatter.4.cloned.1.call-update) | async-done | bytes 12304
  (167 shorter events, 139.6 us)
Async XLA Ops:
  6.5 617.4 %reduce-scatter.4.cloned.1.call-start = ((), (), s32[]{:S(2)}) async-start(), calls=%async_computation.1 | async-start | bytes 3244032
  90.2 7.0 %collective-permute-start = (bf16[16,6144]{1,0:T(8,128)(2,1)S(1)}, bf16[16,6144]{1,0:T(8,128)(2,1)S(1)}, u32[]{:S(2)}, u32[]{:S(2)}) collective-permute-start(bf16[16,6144]{1,0:T(8,128)(2,1)S(1)} %bitcast.283), channel_id=1, source_target_pairs={{480,0},{0,32},{32,64},{64,96},{96,128},{128,160},{160,192},{192,2... | collective-permute-start | bytes 589832 | tf_op jit(solution)/shard_map/ppermute | solution.py:12
  97.1 7.0 %collective-permute-start.2 = (bf16[16,6144]{1,0:T(8,128)(2,1)S(1)}, bf16[16,6144]{1,0:T(8,128)(2,1)S(1)}, u32[]{:S(2)}, u32[]{:S(2)}) collective-permute-start(bf16[16,6144]{1,0:T(8,128)(2,1)S(1)} %collective-permute-done), channel_id=1, source_target_pairs={{480,0},{0,32},{32,64},{64,96},{96,128},{128,160},{160,192},{192,2... | collective-permute-start | bytes 589832 | tf_op jit(solution)/shard_map/ppermute | solution.py:12
  104.1 86.3 %collective-permute-start.4 = (bf16[16,6144]{1,0:T(8,128)(2,1)S(1)}, bf16[16,6144]{1,0:T(8,128)(2,1)S(1)}, u32[]{:S(2)}, u32[]{:S(2)}) collective-permute-start(bf16[16,6144]{1,0:T(8,128)(2,1)S(1)} %collective-permute-done.2), channel_id=1, source_target_pairs={{480,0},{0,32},{32,64},{64,96},{96,128},{128,160},{160,192},{192,2... | collective-permute-start | bytes 589832 | tf_op jit(solution)/shard_map/ppermute | solution.py:12
  188.5 33.8 %collective-permute-start.1 = (bf16[64,6144]{1,0:T(8,128)(2,1)}, bf16[64,6144]{1,0:T(8,128)(2,1)}, u32[]{:S(2)}, u32[]{:S(2)}) collective-permute-start(bf16[64,6144]{1,0:T(8,128)(2,1)} %bitcast.20), channel_id=1, source_target_pairs={{480,0},{0,32},{32,64},{64,96},{96,128},{128,160},{160,192},{192,2... | collective-permute-start | bytes 2359304 | tf_op jit(solution)/shard_map/ppermute | solution.py:12
  190.5 15.1 %collective-permute-start.6 = (bf16[16,6144]{1,0:T(8,128)(2,1)S(1)}, bf16[16,6144]{1,0:T(8,128)(2,1)S(1)}, u32[]{:S(2)}, u32[]{:S(2)}) collective-permute-start(bf16[16,6144]{1,0:T(8,128)(2,1)S(1)} %collective-permute-done.4), channel_id=1, source_target_pairs={{480,0},{0,32},{32,64},{64,96},{96,128},{128,160},{160,192},{192,2... | collective-permute-start | bytes 589832 | tf_op jit(solution)/shard_map/ppermute | solution.py:12
  205.6 22.4 %collective-permute-start.8 = (bf16[16,6144]{1,0:T(8,128)(2,1)S(1)}, bf16[16,6144]{1,0:T(8,128)(2,1)S(1)}, u32[]{:S(2)}, u32[]{:S(2)}) collective-permute-start(bf16[16,6144]{1,0:T(8,128)(2,1)S(1)} %collective-permute-done.6), channel_id=1, source_target_pairs={{480,0},{0,32},{32,64},{64,96},{96,128},{128,160},{160,192},{192,2... | collective-permute-start | bytes 589832 | tf_op jit(solution)/shard_map/ppermute | solution.py:12
  222.3 43.4 %collective-permute-start.3 = (bf16[64,6144]{1,0:T(8,128)(2,1)}, bf16[64,6144]{1,0:T(8,128)(2,1)}, u32[]{:S(2)}, u32[]{:S(2)}) collective-permute-start(bf16[64,6144]{1,0:T(8,128)(2,1)} %collective-permute-done.1), channel_id=1, source_target_pairs={{480,0},{0,32},{32,64},{64,96},{96,128},{128,160},{160,192},{192,2... | collective-permute-start | bytes 2359304 | tf_op jit(solution)/shard_map/ppermute | solution.py:12
  228.0 34.3 %collective-permute-start.10 = (bf16[16,6144]{1,0:T(8,128)(2,1)S(1)}, bf16[16,6144]{1,0:T(8,128)(2,1)}, u32[]{:S(2)}, u32[]{:S(2)}) collective-permute-start(bf16[16,6144]{1,0:T(8,128)(2,1)S(1)} %collective-permute-done.8), channel_id=1, source_target_pairs={{480,0},{0,32},{32,64},{64,96},{96,128},{128,160},{160,192},{192,2... | collective-permute-start | bytes 589832 | tf_op jit(solution)/shard_map/ppermute | solution.py:12
  251.8 33.9 %collective-permute-start.16 = (f32[16,6144]{1,0:T(8,128)S(1)}, f32[16,6144]{1,0:T(8,128)S(1)}, u32[]{:S(2)}, u32[]{:S(2)}) collective-permute-start(f32[16,6144]{1,0:T(8,128)S(1)} %get-tuple-element.1347), channel_id=1, source_target_pairs={{480,0},{0,32},{32,64},{64,96},{96,128},{128,160},{160,192},{192,2... | collective-permute-start | bytes 1179656 | tf_op jit(solution)/shard_map/ppermute | solution.py:12
  262.4 154.0 %collective-permute-start.12 = (bf16[16,6144]{1,0:T(8,128)(2,1)}, bf16[16,6144]{1,0:T(8,128)(2,1)S(1)}, u32[]{:S(2)}, u32[]{:S(2)}) collective-permute-start(bf16[16,6144]{1,0:T(8,128)(2,1)} %collective-permute-done.10), channel_id=1, source_target_pairs={{480,0},{0,32},{32,64},{64,96},{96,128},{128,160},{160,192},{192,2... | collective-permute-start | bytes 589832 | tf_op jit(solution)/shard_map/ppermute | solution.py:12
  267.1 31.8 %collective-permute-start.5 = (bf16[64,6144]{1,0:T(8,128)(2,1)}, bf16[64,6144]{1,0:T(8,128)(2,1)}, u32[]{:S(2)}, u32[]{:S(2)}) collective-permute-start(bf16[64,6144]{1,0:T(8,128)(2,1)} %collective-permute-done.3), channel_id=1, source_target_pairs={{480,0},{0,32},{32,64},{64,96},{96,128},{128,160},{160,192},{192,2... | collective-permute-start | bytes 2359304 | tf_op jit(solution)/shard_map/ppermute | solution.py:12
  285.8 33.2 %collective-permute-start.17 = (f32[16,6144]{1,0:T(8,128)S(1)}, f32[16,6144]{1,0:T(8,128)S(1)}, u32[]{:S(2)}, u32[]{:S(2)}) collective-permute-start(f32[16,6144]{1,0:T(8,128)S(1)} %add.741), channel_id=1, source_target_pairs={{480,0},{0,32},{32,64},{64,96},{96,128},{128,160},{160,192},{192,2... | collective-permute-start | bytes 1179656 | tf_op jit(solution)/shard_map/ppermute | solution.py:12
  300.2 20.7 %collective-permute-start.7 = (bf16[64,6144]{1,0:T(8,128)(2,1)}, bf16[64,6144]{1,0:T(8,128)(2,1)}, u32[]{:S(2)}, u32[]{:S(2)}) collective-permute-start(bf16[64,6144]{1,0:T(8,128)(2,1)} %collective-permute-done.5), channel_id=1, source_target_pairs={{480,0},{0,32},{32,64},{64,96},{96,128},{128,160},{160,192},{192,2... | collective-permute-start | bytes 2359304 | tf_op jit(solution)/shard_map/ppermute | solution.py:12
  319.0 21.1 %collective-permute-start.18 = (f32[16,6144]{1,0:T(8,128)S(1)}, f32[16,6144]{1,0:T(8,128)S(1)}, u32[]{:S(2)}, u32[]{:S(2)}) collective-permute-start(f32[16,6144]{1,0:T(8,128)S(1)} %add.742), channel_id=1, source_target_pairs={{480,0},{0,32},{32,64},{64,96},{96,128},{128,160},{160,192},{192,2... | collective-permute-start | bytes 1179656 | tf_op jit(solution)/shard_map/ppermute | solution.py:12
  322.3 28.8 %collective-permute-start.9 = (bf16[64,6144]{1,0:T(8,128)(2,1)}, bf16[64,6144]{1,0:T(8,128)(2,1)}, u32[]{:S(2)}, u32[]{:S(2)}) collective-permute-start(bf16[64,6144]{1,0:T(8,128)(2,1)} %collective-permute-done.7), channel_id=1, source_target_pairs={{480,0},{0,32},{32,64},{64,96},{96,128},{128,160},{160,192},{192,2... | collective-permute-start | bytes 2359304 | tf_op jit(solution)/shard_map/ppermute | solution.py:12
  340.2 26.5 %collective-permute-start.19 = (f32[16,6144]{1,0:T(8,128)S(1)}, f32[16,6144]{1,0:T(8,128)S(1)}, u32[]{:S(2)}, u32[]{:S(2)}) collective-permute-start(f32[16,6144]{1,0:T(8,128)S(1)} %add.743), channel_id=1, source_target_pairs={{480,0},{0,32},{32,64},{64,96},{96,128},{128,160},{160,192},{192,2... | collective-permute-start | bytes 1179656 | tf_op jit(solution)/shard_map/ppermute | solution.py:12
  352.4 24.9 %collective-permute-start.11 = (bf16[64,6144]{1,0:T(8,128)(2,1)}, bf16[64,6144]{1,0:T(8,128)(2,1)}, u32[]{:S(2)}, u32[]{:S(2)}) collective-permute-start(bf16[64,6144]{1,0:T(8,128)(2,1)} %collective-permute-done.9), channel_id=1, source_target_pairs={{480,0},{0,32},{32,64},{64,96},{96,128},{128,160},{160,192},{192,2... | collective-permute-start | bytes 2359304 | tf_op jit(solution)/shard_map/ppermute | solution.py:12
  366.8 30.0 %collective-permute-start.20 = (f32[16,6144]{1,0:T(8,128)S(1)}, f32[16,6144]{1,0:T(8,128)S(1)}, u32[]{:S(2)}, u32[]{:S(2)}) collective-permute-start(f32[16,6144]{1,0:T(8,128)S(1)} %add.744), channel_id=1, source_target_pairs={{480,0},{0,32},{32,64},{64,96},{96,128},{128,160},{160,192},{192,2... | collective-permute-start | bytes 1179656 | tf_op jit(solution)/shard_map/ppermute | solution.py:12
  378.7 28.7 %collective-permute-start.13 = (bf16[64,6144]{1,0:T(8,128)(2,1)}, bf16[64,6144]{1,0:T(8,128)(2,1)}, u32[]{:S(2)}, u32[]{:S(2)}) collective-permute-start(bf16[64,6144]{1,0:T(8,128)(2,1)} %collective-permute-done.11), channel_id=1, source_target_pairs={{480,0},{0,32},{32,64},{64,96},{96,128},{128,160},{160,192},{192,2... | collective-permute-start | bytes 2359304 | tf_op jit(solution)/shard_map/ppermute | solution.py:12
  396.9 27.7 %collective-permute-start.21 = (f32[16,6144]{1,0:T(8,128)S(1)}, f32[16,6144]{1,0:T(8,128)S(1)}, u32[]{:S(2)}, u32[]{:S(2)}) collective-permute-start(f32[16,6144]{1,0:T(8,128)S(1)} %add.745), channel_id=1, source_target_pairs={{480,0},{0,32},{32,64},{64,96},{96,128},{128,160},{160,192},{192,2... | collective-permute-start | bytes 1179656 | tf_op jit(solution)/shard_map/ppermute | solution.py:12
  407.4 39.3 %collective-permute-start.15 = (bf16[64,6144]{1,0:T(8,128)(2,1)}, bf16[64,6144]{1,0:T(8,128)(2,1)S(1)}, u32[]{:S(2)}, u32[]{:S(2)}) collective-permute-start(bf16[64,6144]{1,0:T(8,128)(2,1)} %collective-permute-done.13), channel_id=1, source_target_pairs={{480,0},{0,32},{32,64},{64,96},{96,128},{128,160},{160,192},{192,2... | collective-permute-start | bytes 2359304 | tf_op jit(solution)/shard_map/ppermute | solution.py:12
  424.7 19.9 %collective-permute-start.22 = (f32[16,6144]{1,0:T(8,128)S(1)}, f32[16,6144]{1,0:T(8,128)S(1)}, u32[]{:S(2)}, u32[]{:S(2)}) collective-permute-start(f32[16,6144]{1,0:T(8,128)S(1)} %add.746), channel_id=1, source_target_pairs={{224,0},{256,32},{288,64},{320,96},{352,128},{384,160},{416,192},{... | collective-permute-start | bytes 1179656 | tf_op jit(solution)/shard_map/ppermute | solution.py:12
  437.7 9.3 %collective-permute-start.14 = (bf16[16,6144]{1,0:T(8,128)(2,1)S(1)}, bf16[16,6144]{1,0:T(8,128)(2,1)S(1)}, u32[]{:S(2)}, u32[]{:S(2)}) collective-permute-start(bf16[16,6144]{1,0:T(8,128)(2,1)S(1)} %get-tuple-element.2353), channel_id=1, source_target_pairs={{480,0},{0,32},{32,64},{64,96},{96,128},{128,160},{160,192},{192,2... | collective-permute-start | bytes 589832 | tf_op jit(solution)/shard_map/ppermute | solution.py:12
  (2 other events, 47.3 us)
Sparse Core Ops, SparseCore 0:
  446.9 177.0 reduce-scatter.3
where the time goes:
time: 634 us; the launch traced here: 632 us
  starting transfers between devices  183 us (29%)
  waiting for transfers between devices  183 us (29%)
  blocking collectives  163 us (26%)
  matrix products  70.1 us (11%)
  between operations  13.9 us (2%)
  other arithmetic  11.8 us (2%)
  local copies, waits for them, and re-layouts  6.36 us (1%)
    ppermute x23, starting transfers between devices, shifted(): return lax.ppermute(block, axis, route)  183 us
    unnamed x2, waiting for transfers between devices  173 us
    all_gather x1, blocking collectives, on_device(): lax.all_gather(probes, 'grp', axis=1, tiled=True)  83.3 us
    all_gather x1, blocking collectives, on_device(): lax.all_gather(points, 'grp', axis=1, tiled=True)  79.9 us
    dot_general x21, matrix products, matern(): lax.dot_general(xa, xb, (((0,), (0,)), ((), ())), preferred_element_type=...  45.8 us
    dot_general x27, matrix products, advance(): lax.dot_general(piece_v, kern, (((1,), (1,)), ((), ())), preferred_elemen...  19.8 us
  transfers between devices with their start and end apart: 24, of which 3 were waited for; matrix products, arithmetic and copies ran while one was open for 14% of the time, Pallas kernels for 0%

commit v1 on v0

v1 whole, which is shorter than its diff:
```python
import math

import jax
import jax.numpy as jnp
from jax import lax
from jax.experimental import pallas as pl
from jax.experimental.pallas import tpu as pltpu
from jax.sharding import PartitionSpec as P

MESH = pl.DeviceIdType.MESH
FEAT, PROBES, OWN = 64, 16, 192
AUX = 16
DEPTH = 128
ROWS = FEAT + AUX + PROBES
PLACES = 32
QUAD = 4 * OWN
PAIR = 2 * OWN
FULL = ((0, 1), (1, 0), (1, 1), (1, 3), (1, 2), (2, 1))
SELF = ((0, 0), (2, 0), (0, 2), (2, 2))
STEPS = FULL + SELF
HOME = len(FULL)
BF = jnp.bfloat16
F32 = jnp.float32


def device(yh, zq, place):
    x, yl, zl, core = place // 8, (place // 4) % 2, (place // 2) % 2, place % 2
    return ((zq // 2) * 8 + x * 2 + core, (yh * 2 + yl) * 4 + (zq % 2) * 2 + zl)


def step_of(slot):
    k = jnp.where(slot >= 18, slot, slot - 3)
    k = jnp.where(slot == 0, 0, k)
    k = jnp.where(slot == 1, 16, k)
    k = jnp.where(slot == 2, 15, k)
    return jnp.where(slot == 3, 17, k)


def entries(m):
    d = jnp.maximum(m, 1e-30)
    t = d * lax.rsqrt(d)
    e = jnp.exp2(t * (-math.sqrt(5.0) * math.log2(math.e)))
    p = (t * (5.0 / 3.0) + math.sqrt(5.0)) * t + 1.0
    return (p * e).astype(BF)


def kernel(scale, pts, prb, out, own, rbuf, cbuf, cpm, cv, rw, rv, yc, yrs, yrr, ycs, ycr,
           rsend, rrecv, csend, crecv, ysend, yrecv, zsend, zrecv):
    loop, grp = lax.axis_index("loop"), lax.axis_index("grp")
    core, x, zhi = loop % 2, (loop // 2) % 4, loop // 8
    y, zlo = grp // 4, grp % 4
    zq, zl, yh, yl = zhi * 2 + zlo // 2, zlo % 2, y // 2, y % 2
    q = ((x * 2 + yl) * 2 + zl) * 2 + core

    barrier = pltpu.get_barrier_semaphore()

    @pl.loop(1, PLACES)
    def _(k):
        pl.semaphore_signal(barrier, inc=1, device_id=device(yh, zq, (q + k) % PLACES), device_id_type=MESH)

    @pl.loop(1, 16)
    def _(k):
        pl.semaphore_signal(barrier, inc=1, device_id=device((yh + k // 4) % 4, (zq + k % 4) % 4, q), device_id_type=MESH)

    own[0:FEAT, :] = pts[...]
    own[FEAT + AUX:ROWS, :] = prb[...]
    wide = pts[...].astype(F32)
    n = jnp.sum(wide * wide, axis=0, keepdims=True)
    hi = n.astype(BF).astype(F32)
    mid = (n - hi).astype(BF).astype(F32)
    lo = n - hi - mid
    row = lax.broadcasted_iota(jnp.int32, (AUX, OWN), 0)
    aux = jnp.where(row == 0, hi, jnp.where(row == 1, mid, jnp.where(row == 2, lo, jnp.where(row < 6, 1.0, 0.0))))
    own[FEAT:FEAT + AUX, :] = aux.astype(BF)
    rbuf[0] = own[...]
    cbuf[HOME] = own[...]
    rw[FEAT + AUX:DEPTH, :] = jnp.zeros((DEPTH - FEAT - AUX, QUAD), BF)
    yc[...] = jnp.zeros_like(yc)

    pl.semaphore_wait(barrier, PLACES - 1 + 15)

    def column_copy(j):
        dy, dz = STEPS[j]
        return pltpu.make_async_remote_copy(
            src_ref=own, dst_ref=cbuf.at[j], send_sem=csend.at[j], recv_sem=crecv.at[j],
            device_id=device((yh - dy + 4) % 4, (zq - dz + 4) % 4, q), device_id_type=MESH)

    def row_copy(s):
        return pltpu.make_async_remote_copy(
            src_ref=own, dst_ref=rbuf.at[s], send_sem=rsend.at[s], recv_sem=rrecv.at[s],
            device_id=device(yh, zq, (q - step_of(s) + PLACES) % PLACES), device_id_type=MESH)

    def row_sum(s):
        return pltpu.make_async_remote_copy(
            src_ref=yrs.at[s], dst_ref=yrr.at[s], send_sem=ysend.at[s], recv_sem=yrecv.at[s],
            device_id=device(yh, zq, (q + step_of(s)) % PLACES), device_id_type=MESH)

    def column_sum(j):
        dy, dz = STEPS[j]
        return pltpu.make_async_remote_copy(
            src_ref=ycs.at[j], dst_ref=ycr.at[j], send_sem=zsend.at[j], recv_sem=zrecv.at[j],
            device_id=device((yh + dy) % 4, (zq + dz) % 4, q), device_id_type=MESH)

    far = [j for j in range(len(STEPS)) if j != HOME]
    for j in far:
        column_copy(j).start()

    @pl.loop(1, PLACES)
    def _(s):
        row_copy(s).start()

    for j in far:
        column_copy(j).wait_recv()

    @pl.loop(0, len(STEPS) // 2)
    def _(h):
        both = jnp.concatenate([cbuf[2 * h].astype(F32), cbuf[2 * h + 1].astype(F32)], axis=1)
        aux = both[FEAT:FEAT + AUX]
        row = lax.broadcasted_iota(jnp.int32, (AUX, PAIR), 0)
        swapped = jnp.where(row < 3, 1.0, jnp.where(row < 6, pltpu.roll(aux, 3, 0), 0.0))
        tall = jnp.concatenate([both[:FEAT] * -2.0, swapped, jnp.zeros((DEPTH - FEAT - AUX, PAIR), F32)], axis=0)
        cpm[pl.ds(pl.multiple_of(h * PAIR, PAIR), PAIR), :] = tall.T.astype(BF)
        cv[h] = both[FEAT + AUX:].astype(BF)

    @pl.loop(0, PLACES // 4)
    def _(quad):
        first = quad * 4

        @pl.when(quad > 0)
        def _():
            row_copy(first).wait_recv()

        for t in range(1, 4):
            row_copy(first + t).wait_recv()
        four = jnp.concatenate([rbuf[first + t].astype(F32) for t in range(4)], axis=1)
        rw[0:FEAT + AUX, :] = four[:FEAT + AUX].astype(BF)
        rv[...] = four[FEAT + AUX:].astype(BF)
        lane = lax.broadcasted_iota(jnp.int32, (PROBES, QUAD), 1)

        def visit(h, acc):
            mine = h >= len(FULL) // 2
            left = jnp.where(jnp.logical_and(mine, quad == 0), 0.5, 1.0)
            right = jnp.where(mine, jnp.where(quad == 0, 0.5, jnp.where(quad == 4, 0.0, 1.0)), 1.0)
            weight = jnp.where(lane < PAIR, left, right)
            vr = (rv[...].astype(F32) * weight).astype(BF)
            cols = cpm[pl.ds(pl.multiple_of(h * PAIR, PAIR), PAIR), :]
            vc = cv[h]
            ysum = yc[h]
            parts = []
            for b in range(3):
                at = slice(b * 256, b * 256 + 256)
                k = entries(jnp.dot(cols, rw[:, at], preferred_element_type=F32))
                parts.append(jnp.dot(vc, k, preferred_element_type=F32))
                ysum = ysum + lax.dot_general(vr[:, at], k, (((1,), (1,)), ((), ())), preferred_element_type=F32)
            yc[h] = ysum
            return acc + jnp.concatenate(parts, axis=1) * weight

        count = jnp.where(quad < 5, len(STEPS) // 2, len(FULL) // 2)
        acc = lax.fori_loop(0, count, visit, jnp.zeros((PROBES, QUAD), F32))
        for t in range(4):
            yrs[first + t] = acc[:, t * OWN:(t + 1) * OWN]

        @pl.when(quad > 0)
        def _():
            row_sum(first).start()

        for t in range(1, 4):
            row_sum(first + t).start()

    for h in range(len(STEPS) // 2):
        ycs[2 * h] = yc[h, :, 0:OWN]
        ycs[2 * h + 1] = yc[h, :, OWN:PAIR]
    for j in far:
        column_sum(j).start()

    total = yrs[0] + ycs[HOME]

    def add_row(s, total):
        row_sum(s).wait_recv()
        return total + yrr[s]

    total = lax.fori_loop(1, PLACES, add_row, total)
    for j in far:
        column_sum(j).wait_recv()
        total = total + ycr[j]
    out[...] = total * scale

    for j in far:
        column_copy(j).wait_send()
        column_sum(j).wait_send()

    @pl.loop(1, PLACES)
    def _(s):
        row_copy(s).wait_send()
        row_sum(s).wait_send()


def on_device(points, probes):
    total = points.shape[1] * lax.axis_size("loop") * lax.axis_size("grp")
    steps = len(STEPS)
    vmem, dma = pltpu.VMEM, pltpu.SemaphoreType.DMA
    return pl.pallas_call(
        lambda *refs: kernel(float(total) ** (-0.5), *refs),
        out_shape=jax.ShapeDtypeStruct((PROBES, OWN), F32),
        in_specs=[pl.BlockSpec(memory_space=vmem)] * 2,
        out_specs=pl.BlockSpec(memory_space=vmem),
        scratch_shapes=[
            vmem((ROWS, OWN), BF),
            vmem((PLACES, ROWS, OWN), BF),
            vmem((steps, ROWS, OWN), BF),
            vmem((steps * OWN, DEPTH), BF),
            vmem((steps // 2, PROBES, PAIR), BF),
            vmem((DEPTH, QUAD), BF),
            vmem((PROBES, QUAD), BF),
            vmem((steps // 2, PROBES, PAIR), F32),
            vmem((PLACES, PROBES, OWN), F32),
            vmem((PLACES, PROBES, OWN), F32),
            vmem((steps, PROBES, OWN), F32),
            vmem((steps, PROBES, OWN), F32),
            dma((PLACES,)), dma((PLACES,)), dma((steps,)), dma((steps,)),
            dma((PLACES,)), dma((PLACES,)), dma((steps,)), dma((steps,)),
        ],
        compiler_params=pltpu.CompilerParams(
            collective_id=0, has_side_effects=True, vmem_limit_bytes=40 * 1024 * 1024
        ),
        name="matern_product",
    )(points, probes)


def solution(mesh):
    specs = P(None, ("loop", "grp"))
    return jax.shard_map(on_device, mesh=mesh, in_specs=(specs, specs), out_specs=specs, check_vma=False)
```

time: 634 us -> 91.8 us (0.14)
  the two profiles are of different devices: /device:TPU:4 before, /device:TPU:8 now
where the time goes in v1:
time: 91.8 us; the launch traced here: 91.6 us
  Pallas kernels  89.5 us (97%)
  local copies, waits for them, and re-layouts  2.06 us (2%)
    pallas_call x1, Pallas kernels, on_device(): pl.pallas_call(lambda *refs: kernel(float(total) ** (-0.5), *refs), out_s...  89.5 us
    unnamed x5, local copies, waits for them, and re-layouts  2.06 us

profile of v1, /device:TPU:8, one launch (start us, length us, event | category | flops | bytes accessed | tf_op | source)
XLA Modules:
  0.0 91.6 jit_solution(2132689718304580955)
XLA Ops:
  0.0 0.0 copy-start
  0.0 0.8 copy-done
  0.8 0.0 copy-start.1
  0.8 0.7 copy-done.1
  1.5 89.5 %matern_product.1 = f32[16,192]{1,0:T(8,128)S(1)} custom-call(bf16[64,192]{1,0:T(8,128)(2,1)S(1)} %copy-done, bf16[16,192]{1,0:T(8,128)(2,1)S(1)} %copy-done.1), custom_call_target="tpu_custom_call" | custom-call | tf_op jit(solution)/shard_map/matern_product/pallas_call | solution.py:202
  90.9 0.6 copy.4
Async XLA Ops:
  0.0 0.8 copy-start
  0.8 0.7 copy-start.1

commit v2 on v0

v2 whole, which is shorter than its diff:
```python
import math

import jax
import jax.numpy as jnp
from jax import lax
from jax.experimental import pallas as pl
from jax.experimental.pallas import tpu as pltpu
from jax.sharding import PartitionSpec as P

MESH = pl.DeviceIdType.MESH
BF = jnp.bfloat16
F32 = jnp.float32
FEAT, PROBES, OWN = 64, 16, 192
AUX = 16
ROWS = FEAT + AUX + PROBES
FOLD = ROWS + ROWS // 2
DEPTH = 3 * FEAT + AUX
PLACES = 16
CHIP = 2 * OWN
LANES = 256
BLOCKS = PLACES * CHIP // LANES
STEPS = (((0, 1), (1, 7), (0, 6), (0, 0), (1, 4)),
         ((1, 2), (0, 3), (1, 5), (1, 0), (0, 4)))
FULL, COLS = 3, 5
BOTH = 14
WORK = BOTH + (BLOCKS - BOTH) * FULL // COLS


def device(xh, z, place, core):
    return ((z // 4 * 4 + xh * 2 + place % 2) * 2 + core, place // 2 * 4 + z % 4)


def tile_of(step, b):
    flat = jnp.maximum(step - BOTH, 0) * COLS + b
    late = step >= BOTH
    return jnp.where(late, flat % FULL, b), jnp.where(late, BOTH + flat // FULL, step)


def weights(h, lb):
    mine = h >= FULL
    half = jnp.logical_or(lb < 2, jnp.logical_or(lb == 12, lb == 13))
    left = jnp.where(jnp.logical_and(mine, half), 0.5, 1.0)
    right = jnp.where(jnp.logical_and(mine, jnp.logical_or(lb == 0, lb == 12)), 0.5, 1.0)
    right = jnp.where(jnp.logical_and(mine, lb == 13), 0.0, right)
    return left, right


def among(value, options):
    hit = value == options[0]
    for option in options[1:]:
        hit = jnp.logical_or(hit, value == option)
    return hit


def tiles_of(halves):
    first, second = halves[0].astype(F32), halves[1].astype(F32)
    low = lax.broadcasted_iota(jnp.int32, (ROWS // 2, 128), 1) < 64
    f0, f1 = first[ROWS:], second[ROWS:]
    top = jnp.where(low, f0, pltpu.roll(f1, 64, 1))
    bottom = jnp.where(low, pltpu.roll(f0, 64, 1), f1)
    return first[:ROWS], jnp.concatenate([top, bottom], axis=0), second[:ROWS]


def kernel(scale, pts, prb, out, own, rbuf, cbuf, cpm, cv, rw, rv, yr, yc, ybuf, zbuf, m, k,
           rsend, rrecv, fsend, frecv, csend, crecv, ysend, yrecv, zsend, zrecv):
    loop, grp = lax.axis_index("loop"), lax.axis_index("grp")
    core, x, z = loop % 2, (loop // 2) % 4, loop // 8 * 4 + grp % 4
    other = 1 - core
    xh, place = x // 2, grp // 4 * 2 + x % 2
    sibling = device(xh, z, place, other)

    def chosen(h):
        (ax, az), (bx, bz) = STEPS[0][h], STEPS[1][h]
        return jnp.where(core == 0, ax, bx), jnp.where(core == 0, az, bz)

    barrier = pltpu.get_barrier_semaphore()
    pl.semaphore_signal(barrier, inc=1, device_id=sibling, device_id_type=MESH)

    @pl.loop(1, 16)
    def _(step):
        for c in range(2):
            pl.semaphore_signal(barrier, inc=1, device_id=device(xh, z, (place + step) % PLACES, c), device_id_type=MESH)
            pl.semaphore_signal(barrier, inc=1, device_id=device((xh + step // 8) % 2, (z + step) % 8, place, c), device_id_type=MESH)

    wide = pts[...].astype(F32)
    n = jnp.sum(wide * wide, axis=0, keepdims=True) * (5.0 / 3.0)
    hi = n.astype(BF).astype(F32)
    mid = (n - hi).astype(BF).astype(F32)
    lo = n - hi - mid
    row = lax.broadcasted_iota(jnp.int32, (AUX, OWN), 0)
    aux = jnp.where(row == 0, hi, jnp.where(row == 1, mid, jnp.where(row == 2, lo, jnp.where(row < 6, 1.0, 0.0))))
    chunk = jnp.concatenate([wide, aux, prb[...].astype(F32)], axis=0)
    own[0:ROWS, :] = chunk[:, :128].astype(BF)
    tail = chunk[:, 128:]
    own[ROWS:FOLD, :] = jnp.concatenate([tail[:ROWS // 2], tail[ROWS // 2:]], axis=1).astype(BF)
    rbuf[0, core] = own[...]
    yr[...] = jnp.zeros_like(yr)
    yc[...] = jnp.zeros_like(yc)
    k[...] = jnp.zeros_like(k)

    pl.semaphore_wait(barrier, 1 + 15 * 4)

    def share():
        return pltpu.make_async_remote_copy(
            src_ref=own, dst_ref=rbuf.at[0, core], send_sem=rsend.at[0], recv_sem=rrecv.at[0, core],
            device_id=sibling, device_id_type=MESH)

    def row_copy(slot, half):
        return pltpu.make_async_remote_copy(
            src_ref=own, dst_ref=rbuf.at[slot, half], send_sem=rsend.at[slot], recv_sem=rrecv.at[slot, half],
            device_id=device(xh, z, (place - slot + PLACES) % PLACES, slot % 2), device_id_type=MESH)

    def forward(slot):
        return pltpu.make_async_remote_copy(
            src_ref=rbuf.at[slot], dst_ref=rbuf.at[slot], send_sem=fsend.at[slot], recv_sem=frecv.at[slot],
            device_id=sibling, device_id_type=MESH)

    def column_copy(taker, h, half):
        dx, dz = STEPS[taker][h]
        return pltpu.make_async_remote_copy(
            src_ref=own, dst_ref=cbuf.at[h, half], send_sem=csend.at[taker, h], recv_sem=crecv.at[h, half],
            device_id=device((xh - dx + 2) % 2, (z - dz + 8) % 8, place, taker), device_id_type=MESH)

    def row_sum(slot, c):
        return pltpu.make_async_remote_copy(
            src_ref=yr.at[pl.ds(slot * 3 + c, 2)], dst_ref=ybuf.at[core, slot],
            send_sem=ysend.at[slot, c], recv_sem=yrecv.at[core, slot],
            device_id=device(xh, z, (place + slot) % PLACES, c), device_id_type=MESH)

    def column_sum(h, c):
        dx, dz = chosen(h)
        return pltpu.make_async_remote_copy(
            src_ref=yc.at[h, pl.ds(c, 2)], dst_ref=zbuf.at[core, h],
            send_sem=zsend.at[h, c], recv_sem=zrecv.at[core, h],
            device_id=device((xh + dx) % 2, (z + dz) % 8, place, c), device_id_type=MESH)

    def arrived(dst, sem):
        pltpu.make_async_remote_copy(
            src_ref=dst, dst_ref=dst, send_sem=fsend.at[0], recv_sem=sem, device_id=sibling, device_id_type=MESH).wait_recv()

    away = [(taker, h) for h in range(COLS) for taker in range(2) if STEPS[taker][h] != (0, 0)]
    share().start()
    row_copy(1, core).start()
    for taker, h in away:
        column_copy(taker, h, core).start()

    @pl.loop(2, PLACES)
    def _(slot):
        row_copy(slot, core).start()

    def hand_over(pair):
        slot = pair * 2 + core
        for half in range(2):
            arrived(rbuf.at[slot, half], rrecv.at[slot, half])
        forward(slot).start()

    def prepare(pair):
        six = tiles_of(rbuf[2 * pair]) + tiles_of(rbuf[2 * pair + 1])
        for b in range(3):
            block = jnp.concatenate([six[2 * b], six[2 * b + 1]], axis=1)
            lb = 3 * pair + b
            feat = block[:FEAT].astype(BF)
            for piece in range(3):
                rw[lb, piece * FEAT:(piece + 1) * FEAT, :] = feat
            rw[lb, 3 * FEAT:, :] = block[FEAT:FEAT + AUX].astype(BF)
            probes = block[FEAT + AUX:]
            left, right = weights(FULL, lb)
            lane = lax.broadcasted_iota(jnp.int32, (PROBES, LANES), 1)
            rv[0, lb] = probes.astype(BF)
            rv[1, lb] = (probes * jnp.where(lane < 128, left, right)).astype(BF)

    arrived(rbuf.at[0, other], rrecv.at[0, other])

    @pl.when(core == 0)
    def _():
        cbuf[FULL] = rbuf[0]

    @pl.when(core == 1)
    def _():
        hand_over(0)

    def column(h, _):
        @pl.when(jnp.logical_or(h != FULL, core == 1))
        def _():
            for half in range(2):
                arrived(cbuf.at[h, half], crecv.at[h, half])
        both = jnp.concatenate(tiles_of(cbuf[h]), axis=1)
        scaled = both[:FEAT] * (-10.0 / 3.0)
        hi = scaled.astype(BF).astype(F32)
        mid = (scaled - hi).astype(BF).astype(F32)
        aux = both[FEAT:FEAT + AUX]
        row = lax.broadcasted_iota(jnp.int32, (AUX, CHIP), 0)
        swapped = jnp.where(row < 3, 1.0, jnp.where(row < 6, pltpu.roll(aux, 3, 0), 0.0))
        cpm[h] = jnp.concatenate([hi, mid, scaled - hi - mid, swapped], axis=0).T.astype(BF)
        cv[h] = both[FEAT + AUX:].astype(BF)
        return 0

    lax.fori_loop(0, COLS, column, 0)

    def cross(step, b):
        h, lb = tile_of(step, b)
        m[b] = jnp.maximum(jnp.dot(cpm[h], rw[lb], preferred_element_type=F32), 1e-30)

    def entries(b):
        d = m[b]
        t = d * lax.rsqrt(d)
        e = jnp.exp2(t * (-math.sqrt(3.0) * math.log2(math.e)))
        p = t + math.sqrt(0.75)
        return ((p * p + 0.25) * e).astype(BF)

    def products(step, b, kern):
        h, lb = tile_of(step, b)
        mine = jnp.where(h >= FULL, 1, 0)
        left, right = weights(h, lb)
        part = jnp.dot(cv[h], kern, preferred_element_type=F32)
        yr[2 * lb] += part[:, :128] * left
        yr[2 * lb + 1] += part[:, 128:] * right
        part = lax.dot_general(rv[mine, lb], kern, (((1,), (1,)), ((), ())), preferred_element_type=F32)
        for tile in range(3):
            yc[h, tile] += part[:, tile * 128:(tile + 1) * 128]

    def send_rows(pair):
        for slot in (2 * pair, 2 * pair + 1):
            @pl.when(slot > 0)
            def _():
                row_sum(slot, 0).start()
                row_sum(slot, 1).start()

            @pl.when(slot == 0)
            def _():
                row_sum(slot, other).start()

    def ready(pair):
        @pl.when(pair < PLACES // 2 - 1)
        def _():
            hand_over(pair + 1)

        slot = pair * 2 + other

        @pl.when(slot > 0)
        def _():
            arrived(rbuf.at[slot], frecv.at[slot])
        prepare(pair)

    ready(0)
    for b in range(COLS):
        cross(0, b)

    def work(step, _):
        late = step + 1 >= BOTH
        starts = jnp.where(late, (step + 1 - BOTH) % 2 == 0, (step + 1) % 3 == 0)

        @pl.when(jnp.logical_and(starts, step + 1 < WORK))
        def _():
            ready(jnp.where(late, 5 + (step + 1 - BOTH) // 2, (step + 1) // 3))

        before, after = jnp.maximum(step - 1, 0), jnp.minimum(step + 1, WORK - 1)
        for b in range(COLS):
            kern = entries(b)
            cross(after, b)
            products(before, b, k[b])
            k[b] = kern

        @pl.when(among(step, (3, 6, 9, 12, 15, 17, 19)))
        def _():
            send_rows(jnp.where(step <= 15, step // 3 - 1, (step - 7) // 2))
        return 0

    lax.fori_loop(0, WORK, work, 0)
    for b in range(COLS):
        products(WORK - 1, b, k[b])
    send_rows(PLACES // 2 - 1)

    for h in range(COLS):
        for c in range(2):
            if STEPS[0][h] == (0, 0):
                @pl.when(jnp.logical_or(core == 1, c == 1))
                def _():
                    column_sum(h, c).start()
            else:
                column_sum(h, c).start()

    total = yr[pl.ds(core, 2)]

    def add_rows(slot, total):
        for c in range(2):
            arrived(ybuf.at[c, slot], yrecv.at[c, slot])
        return total + ybuf[0, slot] + ybuf[1, slot]

    arrived(ybuf.at[other, 0], yrecv.at[other, 0])
    total = total + ybuf[other, 0]
    total = lax.fori_loop(1, PLACES, add_rows, total)
    for taker, h in away:
        arrived(zbuf.at[taker, h], zrecv.at[taker, h])
        total = total + zbuf[taker, h]

    @pl.when(core == 1)
    def _():
        arrived(zbuf.at[0, FULL], zrecv.at[0, FULL])

    @pl.when(core == 0)
    def _():
        zbuf[0, FULL] = yc[FULL, 0:2]

    total = (total + zbuf[0, FULL]) * scale
    main = jnp.where(core == 0, total[0], total[1])
    tail = jnp.where(core == 0, total[1], pltpu.roll(total[0], 64, 1))
    out[:, 0:128] = main
    out[:, 128:OWN] = tail[:, 0:64]

    share().wait_send()
    for taker, h in away:
        column_copy(taker, h, core).wait_send()

    @pl.loop(1, PLACES)
    def _(slot):
        row_copy(slot, core).wait_send()
        row_sum(slot, 0).wait_send()
        row_sum(slot, 1).wait_send()

    row_sum(0, other).wait_send()

    @pl.loop(0, PLACES // 2)
    def _(pair):
        slot = pair * 2 + core

        @pl.when(slot > 0)
        def _():
            forward(slot).wait_send()

    for h in range(COLS):
        for c in range(2):
            if STEPS[0][h] == (0, 0):
                @pl.when(jnp.logical_or(core == 1, c == 1))
                def _():
                    column_sum(h, c).wait_send()
            else:
                column_sum(h, c).wait_send()


def on_device(points, probes):
    total = points.shape[1] * lax.axis_size("loop") * lax.axis_size("grp")
    vmem, dma = pltpu.VMEM, pltpu.SemaphoreType.DMA
    return pl.pallas_call(
        lambda *refs: kernel(float(total) ** (-0.5), *refs),
        out_shape=jax.ShapeDtypeStruct((PROBES, OWN), F32),
        in_specs=[pl.BlockSpec(memory_space=vmem)] * 2,
        out_specs=pl.BlockSpec(memory_space=vmem),
        scratch_shapes=[
            vmem((FOLD, 128), BF),
            vmem((PLACES, 2, FOLD, 128), BF),
            vmem((COLS, 2, FOLD, 128), BF),
            vmem((COLS, CHIP, DEPTH), BF),
            vmem((COLS, PROBES, CHIP), BF),
            vmem((BLOCKS, DEPTH, LANES), BF),
            vmem((2, BLOCKS, PROBES, LANES), BF),
            vmem((PLACES * 3, PROBES, 128), F32),
            vmem((COLS, 3, PROBES, 128), F32),
            vmem((2, PLACES, 2, PROBES, 128), F32),
            vmem((2, COLS, 2, PROBES, 128), F32),
            vmem((COLS, CHIP, LANES), F32),
            vmem((COLS, CHIP, LANES), BF),
            dma((PLACES,)), dma((PLACES, 2)), dma((PLACES,)), dma((PLACES,)), dma((2, COLS)), dma((COLS, 2)),
            dma((PLACES, 2)), dma((2, PLACES)), dma((COLS, 2)), dma((2, COLS)),
        ],
        compiler_params=pltpu.CompilerParams(
            collective_id=0, has_side_effects=True, vmem_limit_bytes=40 * 1024 * 1024
        ),
        name="matern_product",
    )(points, probes)


def solution(mesh):
    specs = P(None, ("loop", "grp"))
    return jax.shard_map(on_device, mesh=mesh, in_specs=(specs, specs), out_specs=specs, check_vma=False)
```

time: 634 us -> 59.7 us (0.09)
  the two profiles are of different devices: /device:TPU:4 before, /device:TPU:1 now
where the time goes in v2:
time: 59.7 us; the launch traced here: 59.5 us
  Pallas kernels  57.4 us (96%)
  local copies, waits for them, and re-layouts  2.06 us (3%)
    pallas_call x1, Pallas kernels, on_device(): pl.pallas_call(lambda *refs: kernel(float(total) ** (-0.5), *refs), out_s...  57.4 us
    unnamed x5, local copies, waits for them, and re-layouts  2.06 us

profile of v2, /device:TPU:1, one launch (start us, length us, event | category | flops | bytes accessed | tf_op | source)
XLA Modules:
  0.0 59.5 jit_solution(3452914192356907738)
XLA Ops:
  0.0 0.0 copy-start
  0.0 0.8 %copy-done = bf16[64,192]{1,0:T(8,128)(2,1)S(1)} copy-done((bf16[64,192]{1,0:T(8,128)(2,1)S(1)}, bf16[64,192]{1,0:T(8,128)(2,1)}, u32[]{:S(2)}) %copy-start) | copy-done | bytes 24600
  0.8 0.0 copy-start.1
  0.8 0.7 %copy-done.1 = bf16[16,192]{1,0:T(8,128)(2,1)S(1)} copy-done((bf16[16,192]{1,0:T(8,128)(2,1)S(1)}, bf16[16,192]{1,0:T(8,128)(2,1)}, u32[]{:S(2)}) %copy-start.1) | copy-done | bytes 6168
  1.5 57.4 %matern_product.1 = f32[16,192]{1,0:T(8,128)S(1)} custom-call(bf16[64,192]{1,0:T(8,128)(2,1)S(1)} %copy-done, bf16[16,192]{1,0:T(8,128)(2,1)S(1)} %copy-done.1), custom_call_target="tpu_custom_call" | custom-call | tf_op jit(solution)/shard_map/matern_product/pallas_call | solution.py:344
  58.9 0.6 %copy.4 = f32[16,192]{1,0:T(8,128)} copy(f32[16,192]{1,0:T(8,128)S(1)} %matern_product.1) | data formatting | bytes 24576
Async XLA Ops:
  0.0 0.8 %copy-start = (bf16[64,192]{1,0:T(8,128)(2,1)S(1)}, bf16[64,192]{1,0:T(8,128)(2,1)}, u32[]{:S(2)}) copy-start(bf16[64,192]{1,0:T(8,128)(2,1)} %refs_0_.1) | copy-start | bytes 73732
  0.8 0.7 %copy-start.1 = (bf16[16,192]{1,0:T(8,128)(2,1)S(1)}, bf16[16,192]{1,0:T(8,128)(2,1)}, u32[]{:S(2)}) copy-start(bf16[16,192]{1,0:T(8,128)(2,1)} %refs_1_.1) | copy-start | bytes 18436

commit v3 on v2

--- a/solution.py
+++ b/solution.py
@@ -19,11 +19,13 @@
 CHIP = 2 * OWN
 LANES = 256
 BLOCKS = PLACES * CHIP // LANES
-STEPS = (((0, 1), (1, 7), (0, 6), (0, 0), (1, 4)),
-         ((1, 2), (0, 3), (1, 5), (1, 0), (0, 4)))
+STEPS = (((0, 1), (0, 6), (1, 7), (0, 0), (1, 4)),
+         ((0, 3), (1, 2), (1, 5), (1, 0), (0, 4)))
 FULL, COLS = 3, 5
+DIRECT = ((1, 3), (0, 0), (1, 0), (0, 1))
+RELAYED = ((1, 1), (0, 2), (1, 2))
 BOTH = 14
-WORK = BOTH + (BLOCKS - BOTH) * FULL // COLS
+WORK = (BOTH * COLS + (BLOCKS - BOTH) * FULL) // COLS
 
 
 def device(xh, z, place, core):
@@ -31,9 +33,11 @@
 
 
 def tile_of(step, b):
-    flat = jnp.maximum(step - BOTH, 0) * COLS + b
-    late = step >= BOTH
-    return jnp.where(late, flat % FULL, b), jnp.where(late, BOTH + flat // FULL, step)
+    flat = step * COLS + b
+    second, third, rest = flat - 2 * BOTH, flat - 4 * BOTH, flat - 5 * BOTH
+    h = jnp.where(second < 0, flat % 2 * 3, jnp.where(third < 0, second % 2 + 1, jnp.where(rest < 0, 4, rest % 3)))
+    lb = jnp.where(second < 0, flat // 2, jnp.where(third < 0, second // 2, jnp.where(rest < 0, third, BOTH + rest // 3)))
+    return h, lb
 
 
 def weights(h, lb):
@@ -61,12 +65,13 @@
     return first[:ROWS], jnp.concatenate([top, bottom], axis=0), second[:ROWS]
 
 
-def kernel(scale, pts, prb, out, own, rbuf, cbuf, cpm, cv, rw, rv, yr, yc, ybuf, zbuf, m, k,
-           rsend, rrecv, fsend, frecv, csend, crecv, ysend, yrecv, zsend, zrecv):
+def kernel(scale, pts, prb, out, own, rbuf, cbuf, cpm, cv, rw, rv, yr, yc, pbuf, ybuf, zbuf, m, k,
+           hsend, hrecv, rsend, rrecv, xsend, xrecv, fsend, frecv, csend, crecv, lsend, lrecv, psend, precv, ysend, yrecv,
+           zsend, zrecv):
     loop, grp = lax.axis_index("loop"), lax.axis_index("grp")
     core, x, z = loop % 2, (loop // 2) % 4, loop // 8 * 4 + grp % 4
     other = 1 - core
-    xh, place = x // 2, grp // 4 * 2 + x % 2
+    xh, xl, place = x // 2, x % 2, grp // 4 * 2 + x % 2
     sibling = device(xh, z, place, other)
 
     def chosen(h):
@@ -102,29 +107,50 @@
 
     def share():
         return pltpu.make_async_remote_copy(
-            src_ref=own, dst_ref=rbuf.at[0, core], send_sem=rsend.at[0], recv_sem=rrecv.at[0, core],
+            src_ref=own, dst_ref=rbuf.at[0, core], send_sem=hsend, recv_sem=hrecv,
             device_id=sibling, device_id_type=MESH)
 
-    def row_copy(slot, half):
-        return pltpu.make_async_remote_copy(
-            src_ref=own, dst_ref=rbuf.at[slot, half], send_sem=rsend.at[slot], recv_sem=rrecv.at[slot, half],
-            device_id=device(xh, z, (place - slot + PLACES) % PLACES, slot % 2), device_id_type=MESH)
+    def row_copy(j):
+        return pltpu.make_async_remote_copy(
+            src_ref=own, dst_ref=rbuf.at[2 * j, core], send_sem=rsend.at[j], recv_sem=rrecv.at[j, core],
+            device_id=device(xh, z, (place - 2 * j + PLACES) % PLACES, j % 2), device_id_type=MESH)
+
+    def across(j):
+        slot = jnp.where(xl == 1, 2 * j + 1, (2 * j + 15) % PLACES)
+        return pltpu.make_async_remote_copy(
+            src_ref=rbuf.at[2 * j], dst_ref=rbuf.at[slot], send_sem=xsend.at[j], recv_sem=xrecv.at[slot],
+            device_id=device(xh, z, place + 1 - 2 * xl, core), device_id_type=MESH)
 
     def forward(slot):
         return pltpu.make_async_remote_copy(
             src_ref=rbuf.at[slot], dst_ref=rbuf.at[slot], send_sem=fsend.at[slot], recv_sem=frecv.at[slot],
             device_id=sibling, device_id_type=MESH)
 
-    def column_copy(taker, h, half):
+    def column_copy(taker, h):
         dx, dz = STEPS[taker][h]
         return pltpu.make_async_remote_copy(
-            src_ref=own, dst_ref=cbuf.at[h, half], send_sem=csend.at[taker, h], recv_sem=crecv.at[h, half],
+            src_ref=own, dst_ref=cbuf.at[h, core], send_sem=csend.at[taker, h], recv_sem=crecv.at[h, core],
             device_id=device((xh - dx + 2) % 2, (z - dz + 8) % 8, place, taker), device_id_type=MESH)
 
+    def relay(taker, h):
+        return pltpu.make_async_remote_copy(
+            src_ref=cbuf.at[3], dst_ref=cbuf.at[h], send_sem=csend.at[taker, h], recv_sem=lrecv.at[h],
+            device_id=device(xh, (z - STEPS[taker][h][1] + 8) % 8, place, taker), device_id_type=MESH)
+
+    def last_relay():
+        return pltpu.make_async_remote_copy(
+            src_ref=cbuf.at[1], dst_ref=cbuf.at[4], send_sem=lsend, recv_sem=lrecv.at[4],
+            device_id=device(xh, (z + jnp.where(core == 0, 2, 6)) % 8, place, other), device_id_type=MESH)
+
+    def trade(pair):
+        return pltpu.make_async_remote_copy(
+            src_ref=yr.at[pl.ds((2 * pair + other) * 3, 3)], dst_ref=pbuf.at[pair], send_sem=psend.at[pair], recv_sem=precv.at[pair],
+            device_id=sibling, device_id_type=MESH)
+
     def row_sum(slot, c):
         return pltpu.make_async_remote_copy(
-            src_ref=yr.at[pl.ds(slot * 3 + c, 2)], dst_ref=ybuf.at[core, slot],
-            send_sem=ysend.at[slot, c], recv_sem=yrecv.at[core, slot],
+            src_ref=yr.at[pl.ds(slot * 3 + c, 2)], dst_ref=ybuf.at[slot],
+            send_sem=ysend.at[slot, c], recv_sem=yrecv.at[slot],
             device_id=device(xh, z, (place + slot) % PLACES, c), device_id_type=MESH)
 
     def column_sum(h, c):
@@ -138,21 +164,38 @@
         pltpu.make_async_remote_copy(
             src_ref=dst, dst_ref=dst, send_sem=fsend.at[0], recv_sem=sem, device_id=sibling, device_id_type=MESH).wait_recv()
 
-    away = [(taker, h) for h in range(COLS) for taker in range(2) if STEPS[taker][h] != (0, 0)]
+    column_copy(*DIRECT[0]).start()
     share().start()
-    row_copy(1, core).start()
-    for taker, h in away:
-        column_copy(taker, h, core).start()
-
-    @pl.loop(2, PLACES)
-    def _(slot):
-        row_copy(slot, core).start()
-
-    def hand_over(pair):
-        slot = pair * 2 + core
-        for half in range(2):
-            arrived(rbuf.at[slot, half], rrecv.at[slot, half])
-        forward(slot).start()
+    for j in (1, 7):
+        row_copy(j).start()
+    for taker, h in DIRECT[1:]:
+        column_copy(taker, h).start()
+    for j in (2, 6, 3, 5, 4):
+        row_copy(j).start()
+
+    def pass_even(j):
+        @pl.when(core == j % 2)
+        def _():
+            for half in range(2):
+                arrived(rbuf.at[2 * j, half], rrecv.at[j, half])
+            forward(2 * j).start()
+            across(j).start()
+
+    def pass_odd(j):
+        @pl.when(core == (j + xl) % 2)
+        def _():
+            arrived(rbuf.at[2 * j + 1], xrecv.at[2 * j + 1])
+            forward(2 * j + 1).start()
+
+    def collect(pair):
+        @pl.when(jnp.logical_and(pair > 0, core != pair % 2))
+        def _():
+            arrived(rbuf.at[2 * pair], frecv.at[2 * pair])
+
+        @pl.when(core != (pair + xl) % 2)
+        def _():
+            arrived(rbuf.at[2 * pair + 1], frecv.at[2 * pair + 1])
+        prepare(pair)
 
     def prepare(pair):
         six = tiles_of(rbuf[2 * pair]) + tiles_of(rbuf[2 * pair + 1])
@@ -169,21 +212,7 @@
             rv[0, lb] = probes.astype(BF)
             rv[1, lb] = (probes * jnp.where(lane < 128, left, right)).astype(BF)
 
-    arrived(rbuf.at[0, other], rrecv.at[0, other])
-
-    @pl.when(core == 0)
-    def _():
-        cbuf[FULL] = rbuf[0]
-
-    @pl.when(core == 1)
-    def _():
-        hand_over(0)
-
-    def column(h, _):
-        @pl.when(jnp.logical_or(h != FULL, core == 1))
-        def _():
-            for half in range(2):
-                arrived(cbuf.at[h, half], crecv.at[h, half])
+    def column(h):
         both = jnp.concatenate(tiles_of(cbuf[h]), axis=1)
         scaled = both[:FEAT] * (-10.0 / 3.0)
         hi = scaled.astype(BF).astype(F32)
@@ -193,9 +222,10 @@
         swapped = jnp.where(row < 3, 1.0, jnp.where(row < 6, pltpu.roll(aux, 3, 0), 0.0))
         cpm[h] = jnp.concatenate([hi, mid, scaled - hi - mid, swapped], axis=0).T.astype(BF)
         cv[h] = both[FEAT + AUX:].astype(BF)
-        return 0
-
-    lax.fori_loop(0, COLS, column, 0)
+
+    def halves(h):
+        for half in range(2):
+            arrived(cbuf.at[h, half], crecv.at[h, half])
 
     def cross(step, b):
         h, lb = tile_of(step, b)
@@ -220,58 +250,17 @@
             yc[h, tile] += part[:, tile * 128:(tile + 1) * 128]
 
     def send_rows(pair):
-        for slot in (2 * pair, 2 * pair + 1):
-            @pl.when(slot > 0)
-            def _():
-                row_sum(slot, 0).start()
-                row_sum(slot, 1).start()
-
-            @pl.when(slot == 0)
-            def _():
-                row_sum(slot, other).start()
-
-    def ready(pair):
-        @pl.when(pair < PLACES // 2 - 1)
-        def _():
-            hand_over(pair + 1)
-
-        slot = pair * 2 + other
+        slot = 2 * pair + core
+        arrived(pbuf.at[pair], precv.at[pair])
+        at = pl.ds(slot * 3, 3)
+        yr[at] = yr[at] + pbuf[pair]
 
         @pl.when(slot > 0)
         def _():
-            arrived(rbuf.at[slot], frecv.at[slot])
-        prepare(pair)
-
-    ready(0)
-    for b in range(COLS):
-        cross(0, b)
-
-    def work(step, _):
-        late = step + 1 >= BOTH
-        starts = jnp.where(late, (step + 1 - BOTH) % 2 == 0, (step + 1) % 3 == 0)
-
-        @pl.when(jnp.logical_and(starts, step + 1 < WORK))
-        def _():
-            ready(jnp.where(late, 5 + (step + 1 - BOTH) // 2, (step + 1) // 3))
-
-        before, after = jnp.maximum(step - 1, 0), jnp.minimum(step + 1, WORK - 1)
-        for b in range(COLS):
-            kern = entries(b)
-            cross(after, b)
-            products(before, b, k[b])
-            k[b] = kern
-
-        @pl.when(among(step, (3, 6, 9, 12, 15, 17, 19)))
-        def _():
-            send_rows(jnp.where(step <= 15, step // 3 - 1, (step - 7) // 2))
-        return 0
-
-    lax.fori_loop(0, WORK, work, 0)
-    for b in range(COLS):
-        products(WORK - 1, b, k[b])
-    send_rows(PLACES // 2 - 1)
-
-    for h in range(COLS):
+            row_sum(slot, 0).start()
+        row_sum(slot, 1).start()
+
+    def send_columns(h):
         for c in range(2):
             if STEPS[0][h] == (0, 0):
                 @pl.when(jnp.logical_or(core == 1, c == 1))
@@ -280,53 +269,165 @@
             else:
                 column_sum(h, c).start()
 
-    total = yr[pl.ds(core, 2)]
+    arrived(rbuf.at[0, other], hrecv)
+
+    @pl.when(core == 0)
+    def _():
+        across(0).start()
+        cbuf[3] = rbuf[0]
+
+    @pl.when(core == 1)
+    def _():
+        halves(3)
+        for taker, h in RELAYED:
+            relay(taker, h).start()
+
+    pass_even(1)
+    pass_odd(0)
+    pass_even(2)
+    pass_odd(1)
+    collect(0)
+    halves(0)
+
+    def first(i, _):
+        column(3 * i)
+        return 0
+
+    lax.fori_loop(0, 2, first, 0)
+    for b in range(COLS):
+        cross(0, b)
+
+    def work(step, _):
+        later = step + 1
+
+        @pl.when(later <= 5)
+        def _():
+            pass_even(later + 2)
+
+        @pl.when(later <= 6)
+        def _():
+            pass_odd(later + 1)
+
+        @pl.when(among(later, (1, 2, 3, 4, 14, 16, 18)))
+        def _():
+            collect(jnp.where(later <= 4, later, (later - 4) // 2))
+
+        @pl.when(later == 5)
+        def _():
+            @pl.when(core == 0)
+            def _():
+                halves(1)
+
+            @pl.when(core == 1)
+            def _():
+                arrived(cbuf.at[1], lrecv.at[1])
+            last_relay().start()
+            arrived(cbuf.at[2], lrecv.at[2])
+
+            def middle(h, _):
+                column(h)
+                return 0
+            lax.fori_loop(1, 3, middle, 0)
+
+        @pl.when(later == 11)
+        def _():
+            arrived(cbuf.at[4], lrecv.at[4])
+            column(4)
+
+        before, after = jnp.maximum(step - 1, 0), jnp.minimum(step + 1, WORK - 1)
+        for b in range(COLS):
+            kern = entries(b)
+            cross(after, b)
+            products(before, b, k[b])
+            k[b] = kern
+
+        for when, pairs in ((12, (0,)), (13, (1, 2)), (14, (3,)), (15, (4,)), (17, (5,)), (19, (6,))):
+            @pl.when(step == when)
+            def _():
+                for pair in pairs:
+                    trade(pair).start()
+
+        for when, pairs in ((13, (0,)), (14, (1, 2)), (15, (3,)), (16, (4,)), (18, (5,))):
+            @pl.when(step == when)
+            def _():
+                for pair in pairs:
+                    send_rows(pair)
+
+        for when, h in ((6, 3), (14, 4)):
+            @pl.when(step == when)
+            def _():
+                send_columns(h)
+        return 0
+
+    lax.fori_loop(0, WORK, work, 0)
+    for b in range(COLS):
+        products(WORK - 1, b, k[b])
+    trade(7).start()
+    for h in (2, 1, 0):
+        send_columns(h)
+    send_rows(6)
+    send_rows(7)
+
+    @pl.when(core == 0)
+    def _():
+        ybuf[0] = yr[0:2]
+        zbuf[0, 3] = yc[3, 0:2]
+
+    @pl.when(core == 1)
+    def _():
+        arrived(ybuf.at[0], yrecv.at[0])
+        arrived(zbuf.at[0, 3], zrecv.at[0, 3])
 
     def add_rows(slot, total):
-        for c in range(2):
-            arrived(ybuf.at[c, slot], yrecv.at[c, slot])
-        return total + ybuf[0, slot] + ybuf[1, slot]
-
-    arrived(ybuf.at[other, 0], yrecv.at[other, 0])
-    total = total + ybuf[other, 0]
-    total = lax.fori_loop(1, PLACES, add_rows, total)
-    for taker, h in away:
-        arrived(zbuf.at[taker, h], zrecv.at[taker, h])
-        total = total + zbuf[taker, h]
-
-    @pl.when(core == 1)
-    def _():
-        arrived(zbuf.at[0, FULL], zrecv.at[0, FULL])
-
-    @pl.when(core == 0)
-    def _():
-        zbuf[0, FULL] = yc[FULL, 0:2]
-
-    total = (total + zbuf[0, FULL]) * scale
+        arrived(ybuf.at[slot], yrecv.at[slot])
+        return total + ybuf[slot]
+
+    total = lax.fori_loop(1, PLACES, add_rows, ybuf[0] + zbuf[0, 3])
+    for h in (3, 4, 2, 1, 0):
+        for taker in range(2):
+            if STEPS[taker][h] != (0, 0):
+                arrived(zbuf.at[taker, h], zrecv.at[taker, h])
+                total = total + zbuf[taker, h]
+    total = total * scale
     main = jnp.where(core == 0, total[0], total[1])
     tail = jnp.where(core == 0, total[1], pltpu.roll(total[0], 64, 1))
     out[:, 0:128] = main
     out[:, 128:OWN] = tail[:, 0:64]
 
     share().wait_send()
-    for taker, h in away:
-        column_copy(taker, h, core).wait_send()
-
-    @pl.loop(1, PLACES)
-    def _(slot):
-        row_copy(slot, core).wait_send()
-        row_sum(slot, 0).wait_send()
-        row_sum(slot, 1).wait_send()
-
-    row_sum(0, other).wait_send()
+    last_relay().wait_send()
+    for taker, h in DIRECT:
+        column_copy(taker, h).wait_send()
+
+    @pl.when(core == 1)
+    def _():
+        for taker, h in RELAYED:
+            relay(taker, h).wait_send()
+
+    @pl.when(core == 0)
+    def _():
+        across(0).wait_send()
+
+    @pl.loop(1, PLACES // 2)
+    def _(j):
+        row_copy(j).wait_send()
+
+        @pl.when(core == j % 2)
+        def _():
+            forward(2 * j).wait_send()
+            across(j).wait_send()
 
     @pl.loop(0, PLACES // 2)
-    def _(pair):
-        slot = pair * 2 + core
-
-        @pl.when(slot > 0)
-        def _():
-            forward(slot).wait_send()
+    def _(j):
+        @pl.when(core == (j + xl) % 2)
+        def _():
+            forward(2 * j + 1).wait_send()
+        trade(j).wait_send()
+
+        @pl.when(2 * j + core > 0)
+        def _():
+            row_sum(2 * j + core, 0).wait_send()
+        row_sum(2 * j + core, 1).wait_send()
 
     for h in range(COLS):
         for c in range(2):
@@ -356,12 +457,14 @@
             vmem((2, BLOCKS, PROBES, LANES), BF),
             vmem((PLACES * 3, PROBES, 128), F32),
             vmem((COLS, 3, PROBES, 128), F32),
-            vmem((2, PLACES, 2, PROBES, 128), F32),
+            vmem((PLACES // 2, 3, PROBES, 128), F32),
+            vmem((PLACES, 2, PROBES, 128), F32),
             vmem((2, COLS, 2, PROBES, 128), F32),
             vmem((COLS, CHIP, LANES), F32),
             vmem((COLS, CHIP, LANES), BF),
-            dma((PLACES,)), dma((PLACES, 2)), dma((PLACES,)), dma((PLACES,)), dma((2, COLS)), dma((COLS, 2)),
-            dma((PLACES, 2)), dma((2, PLACES)), dma((COLS, 2)), dma((2, COLS)),
+            dma, dma, dma((PLACES // 2,)), dma((PLACES // 2, 2)), dma((PLACES // 2,)), dma((PLACES,)),
+            dma((PLACES,)), dma((PLACES,)), dma((2, COLS)), dma((COLS, 2)), dma, dma((COLS,)),
+            dma((PLACES // 2,)), dma((PLACES // 2,)), dma((PLACES, 2)), dma((PLACES,)), dma((COLS, 2)), dma((2, COLS)),
         ],
         compiler_params=pltpu.CompilerParams(
             collective_id=0, has_side_effects=True, vmem_limit_bytes=40 * 1024 * 1024

time: 59.7 us -> 65.1 us (1.090)
  Pallas kernels: 57.4 us -> 62.9 us
    pallas_call x1, Pallas kernels: 57.4 us -> 62.9 us  [on_device(): pl.pallas_call(lambda *refs: kernel(float(total) ** (-0.5), *refs), out_s...]
where the time goes in v3:
time: 65.1 us; the launch traced here: 64.9 us
  Pallas kernels  62.9 us (97%)
  local copies, waits for them, and re-layouts  2.06 us (3%)
    pallas_call x1, Pallas kernels, on_device(): pl.pallas_call(lambda *refs: kernel(float(total) ** (-0.5), *refs), out_s...  62.9 us
    unnamed x5, local copies, waits for them, and re-layouts  2.06 us

profile of v3, /device:TPU:1, one launch (start us, length us, event | category | flops | bytes accessed | tf_op | source)
XLA Modules:
  0.0 64.9 jit_solution(16678447374965436723)
XLA Ops:
  0.0 0.0 copy-start
  0.0 0.8 %copy-done = bf16[64,192]{1,0:T(8,128)(2,1)S(1)} copy-done((bf16[64,192]{1,0:T(8,128)(2,1)S(1)}, bf16[64,192]{1,0:T(8,128)(2,1)}, u32[]{:S(2)}) %copy-start) | copy-done | bytes 24600
  0.8 0.0 copy-start.1
  0.8 0.7 %copy-done.1 = bf16[16,192]{1,0:T(8,128)(2,1)S(1)} copy-done((bf16[16,192]{1,0:T(8,128)(2,1)S(1)}, bf16[16,192]{1,0:T(8,128)(2,1)}, u32[]{:S(2)}) %copy-start.1) | copy-done | bytes 6168
  1.5 62.9 %matern_product.1 = f32[16,192]{1,0:T(8,128)S(1)} custom-call(bf16[64,192]{1,0:T(8,128)(2,1)S(1)} %copy-done, bf16[16,192]{1,0:T(8,128)(2,1)S(1)} %copy-done.1), custom_call_target="tpu_custom_call" | custom-call | tf_op jit(solution)/shard_map/matern_product/pallas_call | solution.py:445
  64.3 0.6 copy.4
Async XLA Ops:
  0.0 0.8 %copy-start = (bf16[64,192]{1,0:T(8,128)(2,1)S(1)}, bf16[64,192]{1,0:T(8,128)(2,1)}, u32[]{:S(2)}) copy-start(bf16[64,192]{1,0:T(8,128)(2,1)} %refs_0_.1) | copy-start | bytes 73732
  0.8 0.7 %copy-start.1 = (bf16[16,192]{1,0:T(8,128)(2,1)S(1)}, bf16[16,192]{1,0:T(8,128)(2,1)}, u32[]{:S(2)}) copy-start(bf16[16,192]{1,0:T(8,128)(2,1)} %refs_1_.1) | copy-start | bytes 18436

commit v4 on v3

--- a/solution.py
+++ b/solution.py
@@ -24,6 +24,7 @@
 FULL, COLS = 3, 5
 DIRECT = ((1, 3), (0, 0), (1, 0), (0, 1))
 RELAYED = ((1, 1), (0, 2), (1, 2))
+NEAR = 9
 BOTH = 14
 WORK = (BOTH * COLS + (BLOCKS - BOTH) * FULL) // COLS
 
@@ -34,17 +35,29 @@
 
 def tile_of(step, b):
     flat = step * COLS + b
-    second, third, rest = flat - 2 * BOTH, flat - 4 * BOTH, flat - 5 * BOTH
-    h = jnp.where(second < 0, flat % 2 * 3, jnp.where(third < 0, second % 2 + 1, jnp.where(rest < 0, 4, rest % 3)))
-    lb = jnp.where(second < 0, flat // 2, jnp.where(third < 0, second // 2, jnp.where(rest < 0, third, BOTH + rest // 3)))
-    return h, lb
+    two, three = flat - 2 * NEAR, flat - 4 * NEAR
+    four = three - COLS * (BOTH - NEAR)
+    rest = four - NEAR
+    all5 = jnp.maximum(three, 0) % 5
+    all5 = jnp.where(all5 == 1, 3, jnp.where(jnp.logical_or(all5 == 2, all5 == 3), all5 - 1, all5))
+    h = jnp.where(rest < 0, 4, rest % 3)
+    h = jnp.where(three < 0, two % 2 + 1, jnp.where(four < 0, all5, h))
+    lb = jnp.where(rest < 0, four, BOTH + rest // 3)
+    lb = jnp.where(three < 0, two // 2, jnp.where(four < 0, NEAR + three // 5, lb))
+    return jnp.where(two < 0, flat % 2 * 3, h), jnp.where(two < 0, flat // 2, lb)
+
+
+def chip_step(pos):
+    step = jnp.where(pos < 3, 2 * pos, jnp.where(pos < 10, 2 * pos - 5, pos - 1))
+    step = jnp.where(pos == 4, 6, jnp.where(pos == 5, 3, jnp.where(pos == 6, 5, step)))
+    step = jnp.where(pos == 7, 8, jnp.where(pos == 8, 7, jnp.where(pos == 9, 14, step)))
+    return jnp.where(pos == 15, 15, step)
 
 
 def weights(h, lb):
     mine = h >= FULL
-    half = jnp.logical_or(lb < 2, jnp.logical_or(lb == 12, lb == 13))
-    left = jnp.where(jnp.logical_and(mine, half), 0.5, 1.0)
-    right = jnp.where(jnp.logical_and(mine, jnp.logical_or(lb == 0, lb == 12)), 0.5, 1.0)
+    left = jnp.where(jnp.logical_and(mine, among(lb, (0, 1, 11))), 0.5, 1.0)
+    right = jnp.where(jnp.logical_and(mine, among(lb, (0, 10, 11))), 0.5, 1.0)
     right = jnp.where(jnp.logical_and(mine, lb == 13), 0.0, right)
     return left, right
 
@@ -65,9 +78,9 @@
     return first[:ROWS], jnp.concatenate([top, bottom], axis=0), second[:ROWS]
 
 
-def kernel(scale, pts, prb, out, own, rbuf, cbuf, cpm, cv, rw, rv, yr, yc, pbuf, ybuf, zbuf, m, k,
-           hsend, hrecv, rsend, rrecv, xsend, xrecv, fsend, frecv, csend, crecv, lsend, lrecv, psend, precv, ysend, yrecv,
-           zsend, zrecv):
+def kernel(scale, points, probes, out, pts, prb, own, rbuf, cbuf, cpm, cv, rw, rv, yr, yc, pbuf, ybuf, zbuf, m, k,
+           hsend, hrecv, asend, arecv, rsend, rrecv, xsend, xrecv, fsend, frecv, csend, crecv, lsend, lrecv, psend, precv, ysend, yrecv,
+           zsend, zrecv, isem):
     loop, grp = lax.axis_index("loop"), lax.axis_index("grp")
     core, x, z = loop % 2, (loop // 2) % 4, loop // 8 * 4 + grp % 4
     other = 1 - core
@@ -86,6 +99,15 @@
         for c in range(2):
             pl.semaphore_signal(barrier, inc=1, device_id=device(xh, z, (place + step) % PLACES, c), device_id_type=MESH)
             pl.semaphore_signal(barrier, inc=1, device_id=device((xh + step // 8) % 2, (z + step) % 8, place, c), device_id_type=MESH)
+
+    copies = [pltpu.make_async_copy(points, pts, isem.at[0]), pltpu.make_async_copy(probes, prb, isem.at[1])]
+    for copy in copies:
+        copy.start()
+    yr[...] = jnp.zeros_like(yr)
+    yc[...] = jnp.zeros_like(yc)
+    k[...] = jnp.zeros_like(k)
+    for copy in copies:
+        copy.wait()
 
     wide = pts[...].astype(F32)
     n = jnp.sum(wide * wide, axis=0, keepdims=True) * (5.0 / 3.0)
@@ -99,9 +121,6 @@
     tail = chunk[:, 128:]
     own[ROWS:FOLD, :] = jnp.concatenate([tail[:ROWS // 2], tail[ROWS // 2:]], axis=1).astype(BF)
     rbuf[0, core] = own[...]
-    yr[...] = jnp.zeros_like(yr)
-    yc[...] = jnp.zeros_like(yc)
-    k[...] = jnp.zeros_like(k)
 
     pl.semaphore_wait(barrier, 1 + 15 * 4)
 
@@ -121,6 +140,11 @@
             src_ref=rbuf.at[2 * j], dst_ref=rbuf.at[slot], send_sem=xsend.at[j], recv_sem=xrecv.at[slot],
             device_id=device(xh, z, place + 1 - 2 * xl, core), device_id_type=MESH)
 
+    def around():
+        return pltpu.make_async_remote_copy(
+            src_ref=rbuf.at[12], dst_ref=rbuf.at[8], send_sem=asend, recv_sem=arecv,
+            device_id=device(xh, z, (place + 4) % PLACES, 0), device_id_type=MESH)
+
     def forward(slot):
         return pltpu.make_async_remote_copy(
             src_ref=rbuf.at[slot], dst_ref=rbuf.at[slot], send_sem=fsend.at[slot], recv_sem=frecv.at[slot],
@@ -147,11 +171,11 @@
             src_ref=yr.at[pl.ds((2 * pair + other) * 3, 3)], dst_ref=pbuf.at[pair], send_sem=psend.at[pair], recv_sem=precv.at[pair],
             device_id=sibling, device_id_type=MESH)
 
-    def row_sum(slot, c):
-        return pltpu.make_async_remote_copy(
-            src_ref=yr.at[pl.ds(slot * 3 + c, 2)], dst_ref=ybuf.at[slot],
-            send_sem=ysend.at[slot, c], recv_sem=yrecv.at[slot],
-            device_id=device(xh, z, (place + slot) % PLACES, c), device_id_type=MESH)
+    def row_sum(pos, c):
+        return pltpu.make_async_remote_copy(
+            src_ref=yr.at[pl.ds(pos * 3 + c, 2)], dst_ref=ybuf.at[pos],
+            send_sem=ysend.at[pos, c], recv_sem=yrecv.at[pos],
+            device_id=device(xh, z, (place + chip_step(pos)) % PLACES, c), device_id_type=MESH)
 
     def column_sum(h, c):
         dx, dz = chosen(h)
@@ -164,20 +188,28 @@
         pltpu.make_async_remote_copy(
             src_ref=dst, dst_ref=dst, send_sem=fsend.at[0], recv_sem=sem, device_id=sibling, device_id_type=MESH).wait_recv()
 
-    column_copy(*DIRECT[0]).start()
     share().start()
-    for j in (1, 7):
-        row_copy(j).start()
-    for taker, h in DIRECT[1:]:
-        column_copy(taker, h).start()
-    for j in (2, 6, 3, 5, 4):
+    row_copy(1).start()
+    column_copy(1, 3).start()
+    column_copy(0, 0).start()
+    row_copy(2).start()
+    column_copy(1, 0).start()
+    row_copy(3).start()
+    row_copy(6).start()
+    column_copy(0, 1).start()
+    for j in (7, 5):
         row_copy(j).start()
 
     def pass_even(j):
         @pl.when(core == j % 2)
         def _():
-            for half in range(2):
-                arrived(rbuf.at[2 * j, half], rrecv.at[j, half])
+            if j == 4:
+                arrived(rbuf.at[8], arecv)
+            else:
+                for half in range(2):
+                    arrived(rbuf.at[2 * j, half], rrecv.at[j, half])
+            if j == 6:
+                around().start()
             forward(2 * j).start()
             across(j).start()
 
@@ -188,17 +220,17 @@
             forward(2 * j + 1).start()
 
     def collect(pair):
-        @pl.when(jnp.logical_and(pair > 0, core != pair % 2))
-        def _():
-            arrived(rbuf.at[2 * pair], frecv.at[2 * pair])
-
-        @pl.when(core != (pair + xl) % 2)
-        def _():
-            arrived(rbuf.at[2 * pair + 1], frecv.at[2 * pair + 1])
+        for t in range(2):
+            slot = chip_step(2 * pair + t)
+            j, odd = slot // 2, slot % 2
+
+            @pl.when(jnp.logical_and(slot > 0, core != (j + odd * xl) % 2))
+            def _():
+                arrived(rbuf.at[slot], frecv.at[slot])
         prepare(pair)
 
     def prepare(pair):
-        six = tiles_of(rbuf[2 * pair]) + tiles_of(rbuf[2 * pair + 1])
+        six = tiles_of(rbuf[chip_step(2 * pair)]) + tiles_of(rbuf[chip_step(2 * pair + 1)])
         for b in range(3):
             block = jnp.concatenate([six[2 * b], six[2 * b + 1]], axis=1)
             lb = 3 * pair + b
@@ -283,9 +315,11 @@
             relay(taker, h).start()
 
     pass_even(1)
-    pass_odd(0)
-    pass_even(2)
-    pass_odd(1)
+
+    @pl.when(core == 0)
+    def _():
+        halves(1)
+        last_relay().start()
     collect(0)
     halves(0)
 
@@ -294,46 +328,11 @@
         return 0
 
     lax.fori_loop(0, 2, first, 0)
+    pass_even(2)
     for b in range(COLS):
         cross(0, b)
 
-    def work(step, _):
-        later = step + 1
-
-        @pl.when(later <= 5)
-        def _():
-            pass_even(later + 2)
-
-        @pl.when(later <= 6)
-        def _():
-            pass_odd(later + 1)
-
-        @pl.when(among(later, (1, 2, 3, 4, 14, 16, 18)))
-        def _():
-            collect(jnp.where(later <= 4, later, (later - 4) // 2))
-
-        @pl.when(later == 5)
-        def _():
-            @pl.when(core == 0)
-            def _():
-                halves(1)
-
-            @pl.when(core == 1)
-            def _():
-                arrived(cbuf.at[1], lrecv.at[1])
-            last_relay().start()
-            arrived(cbuf.at[2], lrecv.at[2])
-
-            def middle(h, _):
-                column(h)
-                return 0
-            lax.fori_loop(1, 3, middle, 0)
-
-        @pl.when(later == 11)
-        def _():
-            arrived(cbuf.at[4], lrecv.at[4])
-            column(4)
-
+    def tiles(step):
         before, after = jnp.maximum(step - 1, 0), jnp.minimum(step + 1, WORK - 1)
         for b in range(COLS):
             kern = entries(b)
@@ -341,25 +340,72 @@
             products(before, b, k[b])
             k[b] = kern
 
-        for when, pairs in ((12, (0,)), (13, (1, 2)), (14, (3,)), (15, (4,)), (17, (5,)), (19, (6,))):
-            @pl.when(step == when)
+    def work(step, _):
+        later = step + 1
+
+        def arrivals(events):
+            for when, evens, odds, pairs in events:
+                @pl.when(later == when)
+                def _():
+                    for j in evens:
+                        pass_even(j)
+                    for j in odds:
+                        pass_odd(j)
+                    for pair in pairs:
+                        collect(pair)
+
+        @pl.when(later < 8)
+        def _():
+            arrivals(((1, (6,), (0,), (1,)), (2, (3,), (1,), (2,)), (3, (7,), (), ()), (4, (5,), (), ()), (5, (4,), (), ()),
+                      (6, (), (2,), ()), (7, (), (), (3,))))
+
+            @pl.when(later == 3)
             def _():
-                for pair in pairs:
+                @pl.when(core == 1)
+                def _():
+                    arrived(cbuf.at[1], lrecv.at[1])
+                    last_relay().start()
+                arrived(cbuf.at[2], lrecv.at[2])
+
+                def middle(h, _):
+                    column(h)
+                    return 0
+                lax.fori_loop(1, 3, middle, 0)
+
+        @pl.when(later >= 8)
+        def _():
+            arrivals(((9, (), (3, 4, 5), ()), (10, (), (6, 7), (4,))))
+
+            @pl.when(later == 8)
+            def _():
+                arrived(cbuf.at[4], lrecv.at[4])
+                column(4)
+
+        tiles(step)
+        return 0
+
+    def work_two(half, _):
+        for when, pair in ((6, 5), (7, 6), (8, 7)):
+            @pl.when(half == when)
+            def _():
+                collect(pair)
+
+        tiles(2 * half)
+        tiles(2 * half + 1)
+        for when, trades, sends, chunks in ((5, (3,), (), ()), (6, (0,), (3,), (3,)), (7, (1, 2, 4), (0,), (4,)), (8, (5,), (1, 2, 4), ()),
+                                            (9, (6,), (5,), ())):
+            @pl.when(half == when)
+            def _():
+                for pair in trades:
                     trade(pair).start()
-
-        for when, pairs in ((13, (0,)), (14, (1, 2)), (15, (3,)), (16, (4,)), (18, (5,))):
-            @pl.when(step == when)
-            def _():
-                for pair in pairs:
+                for pair in sends:
                     send_rows(pair)
-
-        for when, h in ((6, 3), (14, 4)):
-            @pl.when(step == when)
-            def _():
-                send_columns(h)
+                for h in chunks:
+                    send_columns(h)
         return 0
 
-    lax.fori_loop(0, WORK, work, 0)
+    lax.fori_loop(0, WORK // 2, work, 0)
+    lax.fori_loop(WORK // 4, WORK // 2, work_two, 0)
     for b in range(COLS):
         products(WORK - 1, b, k[b])
     trade(7).start()
@@ -367,6 +413,56 @@
         send_columns(h)
     send_rows(6)
     send_rows(7)
+
+    share().wait_send()
+    last_relay().wait_send()
+    for taker, h in DIRECT:
+        column_copy(taker, h).wait_send()
+
+    @pl.when(core == 1)
+    def _():
+        for taker, h in RELAYED:
+            relay(taker, h).wait_send()
+
+    @pl.when(core == 0)
+    def _():
+        across(0).wait_send()
+        around().wait_send()
+
+    @pl.loop(1, PLACES // 2)
+    def _(j):
+        @pl.when(j != 4)
+        def _():
+            row_copy(j).wait_send()
+
+        @pl.when(core == j % 2)
+        def _():
+            forward(2 * j).wait_send()
+            across(j).wait_send()
+
+    @pl.loop(0, PLACES // 2)
+    def _(j):
+        @pl.when(core == (j + xl) % 2)
+        def _():
+            forward(2 * j + 1).wait_send()
+
+    @pl.loop(0, PLACES // 2)
+    def _(j):
+        trade(j).wait_send()
+
+        @pl.when(2 * j + core > 0)
+        def _():
+            row_sum(2 * j + core, 0).wait_send()
+        row_sum(2 * j + core, 1).wait_send()
+
+    for h in range(COLS):
+        for c in range(2):
+            if STEPS[0][h] == (0, 0):
+                @pl.when(jnp.logical_or(core == 1, c == 1))
+                def _():
+                    column_sum(h, c).wait_send()
+            else:
+                column_sum(h, c).wait_send()
 
     @pl.when(core == 0)
     def _():
@@ -394,50 +490,6 @@
     out[:, 0:128] = main
     out[:, 128:OWN] = tail[:, 0:64]
 
-    share().wait_send()
-    last_relay().wait_send()
-    for taker, h in DIRECT:
-        column_copy(taker, h).wait_send()
-
-    @pl.when(core == 1)
-    def _():
-        for taker, h in RELAYED:
-            relay(taker, h).wait_send()
-
-    @pl.when(core == 0)
-    def _():
-        across(0).wait_send()
-
-    @pl.loop(1, PLACES // 2)
-    def _(j):
-        row_copy(j).wait_send()
-
-        @pl.when(core == j % 2)
-        def _():
-            forward(2 * j).wait_send()
-            across(j).wait_send()
-
-    @pl.loop(0, PLACES // 2)
-    def _(j):
-        @pl.when(core == (j + xl) % 2)
-        def _():
-            forward(2 * j + 1).wait_send()
-        trade(j).wait_send()
-
-        @pl.when(2 * j + core > 0)
-        def _():
-            row_sum(2 * j + core, 0).wait_send()
-        row_sum(2 * j + core, 1).wait_send()
-
-    for h in range(COLS):
-        for c in range(2):
-            if STEPS[0][h] == (0, 0):
-                @pl.when(jnp.logical_or(core == 1, c == 1))
-                def _():
-                    column_sum(h, c).wait_send()
-            else:
-                column_sum(h, c).wait_send()
-
 
 def on_device(points, probes):
     total = points.shape[1] * lax.axis_size("loop") * lax.axis_size("grp")
@@ -445,9 +497,11 @@
     return pl.pallas_call(
         lambda *refs: kernel(float(total) ** (-0.5), *refs),
         out_shape=jax.ShapeDtypeStruct((PROBES, OWN), F32),
-        in_specs=[pl.BlockSpec(memory_space=vmem)] * 2,
+        in_specs=[pl.BlockSpec(memory_space=pltpu.HBM)] * 2,
         out_specs=pl.BlockSpec(memory_space=vmem),
         scratch_shapes=[
+            vmem((FEAT, OWN), BF),
+            vmem((PROBES, OWN), BF),
             vmem((FOLD, 128), BF),
             vmem((PLACES, 2, FOLD, 128), BF),
             vmem((COLS, 2, FOLD, 128), BF),
@@ -462,9 +516,9 @@
             vmem((2, COLS, 2, PROBES, 128), F32),
             vmem((COLS, CHIP, LANES), F32),
             vmem((COLS, CHIP, LANES), BF),
-            dma, dma, dma((PLACES // 2,)), dma((PLACES // 2, 2)), dma((PLACES // 2,)), dma((PLACES,)),
+            dma, dma, dma, dma, dma((PLACES // 2,)), dma((PLACES // 2, 2)), dma((PLACES // 2,)), dma((PLACES,)),
             dma((PLACES,)), dma((PLACES,)), dma((2, COLS)), dma((COLS, 2)), dma, dma((COLS,)),
-            dma((PLACES // 2,)), dma((PLACES // 2,)), dma((PLACES, 2)), dma((PLACES,)), dma((COLS, 2)), dma((2, COLS)),
+            dma((PLACES // 2,)), dma((PLACES // 2,)), dma((PLACES, 2)), dma((PLACES,)), dma((COLS, 2)), dma((2, COLS)), dma((2,)),
         ],
         compiler_params=pltpu.CompilerParams(
             collective_id=0, has_side_effects=True, vmem_limit_bytes=40 * 1024 * 1024

time: 65.1 us -> 56.7 us (0.87)
  Pallas kernels: 62.9 us -> 54.5 us
    pallas_call x1, Pallas kernels: 62.9 us -> 54.5 us  [on_device(): pl.pallas_call(lambda *refs: kernel(float(total) ** (-0.5), *refs), out_s...]
where the time goes in v4:
time: 56.7 us; the launch traced here: 56.5 us
  Pallas kernels  54.5 us (96%)
  local copies, waits for them, and re-layouts  2.06 us (4%)
    pallas_call x1, Pallas kernels, on_device(): pl.pallas_call(lambda *refs: kernel(float(total) ** (-0.5), *refs), out_s...  54.5 us
    unnamed x5, local copies, waits for them, and re-layouts  2.06 us

profile of v4, /device:TPU:1, one launch (start us, length us, event | category | flops | bytes accessed | tf_op | source)
XLA Modules:
  0.0 56.5 jit_solution(3591352508403950751)
XLA Ops:
  0.0 0.0 copy-start
  0.0 0.8 %copy-done = bf16[64,192]{1,0:T(8,128)(2,1)S(1)} copy-done((bf16[64,192]{1,0:T(8,128)(2,1)S(1)}, bf16[64,192]{1,0:T(8,128)(2,1)}, u32[]{:S(2)}) %copy-start) | copy-done | bytes 24600
  0.8 0.0 copy-start.1
  0.8 0.7 %copy-done.1 = bf16[16,192]{1,0:T(8,128)(2,1)S(1)} copy-done((bf16[16,192]{1,0:T(8,128)(2,1)S(1)}, bf16[16,192]{1,0:T(8,128)(2,1)}, u32[]{:S(2)}) %copy-start.1) | copy-done | bytes 6168
  1.5 54.5 %matern_product.1 = f32[16,192]{1,0:T(8,128)S(1)} custom-call(bf16[64,192]{1,0:T(8,128)(2,1)S(1)} %copy-done, bf16[16,192]{1,0:T(8,128)(2,1)S(1)} %copy-done.1), custom_call_target="tpu_custom_call" | custom-call | tf_op jit(solution)/shard_map/matern_product/pallas_call | solution.py:497
  55.9 0.6 %copy.4 = f32[16,192]{1,0:T(8,128)} copy(f32[16,192]{1,0:T(8,128)S(1)} %matern_product.1) | data formatting | bytes 24576
Async XLA Ops:
  0.0 0.8 %copy-start = (bf16[64,192]{1,0:T(8,128)(2,1)S(1)}, bf16[64,192]{1,0:T(8,128)(2,1)}, u32[]{:S(2)}) copy-start(bf16[64,192]{1,0:T(8,128)(2,1)} %refs_0_.1) | copy-start | bytes 73732
  0.8 0.7 %copy-start.1 = (bf16[16,192]{1,0:T(8,128)(2,1)S(1)}, bf16[16,192]{1,0:T(8,128)(2,1)}, u32[]{:S(2)}) copy-start(bf16[16,192]{1,0:T(8,128)(2,1)} %refs_1_.1) | copy-start | bytes 18436

commit v5 on v4

--- a/solution.py
+++ b/solution.py
@@ -24,7 +24,7 @@
 FULL, COLS = 3, 5
 DIRECT = ((1, 3), (0, 0), (1, 0), (0, 1))
 RELAYED = ((1, 1), (0, 2), (1, 2))
-NEAR = 9
+NEAR, NEXT = 9, 12
 BOTH = 14
 WORK = (BOTH * COLS + (BLOCKS - BOTH) * FULL) // COLS
 
@@ -36,14 +36,16 @@
 def tile_of(step, b):
     flat = step * COLS + b
     two, three = flat - 2 * NEAR, flat - 4 * NEAR
-    four = three - COLS * (BOTH - NEAR)
-    rest = four - NEAR
-    all5 = jnp.maximum(three, 0) % 5
-    all5 = jnp.where(all5 == 1, 3, jnp.where(jnp.logical_or(all5 == 2, all5 == 3), all5 - 1, all5))
-    h = jnp.where(rest < 0, 4, rest % 3)
-    h = jnp.where(three < 0, two % 2 + 1, jnp.where(four < 0, all5, h))
-    lb = jnp.where(rest < 0, four, BOTH + rest // 3)
-    lb = jnp.where(three < 0, two // 2, jnp.where(four < 0, NEAR + three // 5, lb))
+    four = three - COLS * (NEXT - NEAR)
+    five = four - NEAR
+    rest = five - COLS * (BOTH - NEXT)
+    turn = jnp.where(four < 0, three, five) % 5
+    turn = jnp.where(turn == 1, 3, jnp.where(jnp.logical_or(turn == 2, turn == 3), turn - 1, turn))
+    h = jnp.where(rest < 0, turn, rest % 3)
+    h = jnp.where(jnp.logical_and(four >= 0, five < 0), 4, jnp.where(three < 0, two % 2 + 1, h))
+    lb = jnp.where(rest < 0, NEXT + five // 5, BOTH + rest // 3)
+    lb = jnp.where(four < 0, NEAR + three // 5, jnp.where(five < 0, four, lb))
+    lb = jnp.where(three < 0, two // 2, lb)
     return jnp.where(two < 0, flat % 2 * 3, h), jnp.where(two < 0, flat // 2, lb)
 
 
@@ -131,13 +133,13 @@
 
     def row_copy(j):
         return pltpu.make_async_remote_copy(
-            src_ref=own, dst_ref=rbuf.at[2 * j, core], send_sem=rsend.at[j], recv_sem=rrecv.at[j, core],
+            src_ref=own, dst_ref=rbuf.at[2 * j, core], send_sem=rsend.at[j], recv_sem=rrecv.at[j // 2, core],
             device_id=device(xh, z, (place - 2 * j + PLACES) % PLACES, j % 2), device_id_type=MESH)
 
     def across(j):
         slot = jnp.where(xl == 1, 2 * j + 1, (2 * j + 15) % PLACES)
         return pltpu.make_async_remote_copy(
-            src_ref=rbuf.at[2 * j], dst_ref=rbuf.at[slot], send_sem=xsend.at[j], recv_sem=xrecv.at[slot],
+            src_ref=rbuf.at[2 * j], dst_ref=rbuf.at[slot], send_sem=xsend.at[j // 2], recv_sem=xrecv.at[slot // 4],
             device_id=device(xh, z, place + 1 - 2 * xl, core), device_id_type=MESH)
 
     def around():
@@ -147,7 +149,7 @@
 
     def forward(slot):
         return pltpu.make_async_remote_copy(
-            src_ref=rbuf.at[slot], dst_ref=rbuf.at[slot], send_sem=fsend.at[slot], recv_sem=frecv.at[slot],
+            src_ref=rbuf.at[slot], dst_ref=rbuf.at[slot], send_sem=fsend.at[slot % 2 * 4 + slot // 4], recv_sem=frecv.at[slot % 2 * 4 + slot // 4],
             device_id=sibling, device_id_type=MESH)
 
     def column_copy(taker, h):
@@ -158,12 +160,12 @@
 
     def relay(taker, h):
         return pltpu.make_async_remote_copy(
-            src_ref=cbuf.at[3], dst_ref=cbuf.at[h], send_sem=csend.at[taker, h], recv_sem=lrecv.at[h],
+            src_ref=cbuf.at[3], dst_ref=cbuf.at[h], send_sem=csend.at[taker, h], recv_sem=lrecv.at[h // 2],
             device_id=device(xh, (z - STEPS[taker][h][1] + 8) % 8, place, taker), device_id_type=MESH)
 
     def last_relay():
         return pltpu.make_async_remote_copy(
-            src_ref=cbuf.at[1], dst_ref=cbuf.at[4], send_sem=lsend, recv_sem=lrecv.at[4],
+            src_ref=cbuf.at[1], dst_ref=cbuf.at[4], send_sem=lsend, recv_sem=lrecv.at[2],
             device_id=device(xh, (z + jnp.where(core == 0, 2, 6)) % 8, place, other), device_id_type=MESH)
 
     def trade(pair):
@@ -174,7 +176,7 @@
     def row_sum(pos, c):
         return pltpu.make_async_remote_copy(
             src_ref=yr.at[pl.ds(pos * 3 + c, 2)], dst_ref=ybuf.at[pos],
-            send_sem=ysend.at[pos, c], recv_sem=yrecv.at[pos],
+            send_sem=ysend.at[pos // 2, c], recv_sem=yrecv.at[pos],
             device_id=device(xh, z, (place + chip_step(pos)) % PLACES, c), device_id_type=MESH)
 
     def column_sum(h, c):
@@ -207,7 +209,7 @@
                 arrived(rbuf.at[8], arecv)
             else:
                 for half in range(2):
-                    arrived(rbuf.at[2 * j, half], rrecv.at[j, half])
+                    arrived(rbuf.at[2 * j, half], rrecv.at[j // 2, half])
             if j == 6:
                 around().start()
             forward(2 * j).start()
@@ -216,7 +218,7 @@
     def pass_odd(j):
         @pl.when(core == (j + xl) % 2)
         def _():
-            arrived(rbuf.at[2 * j + 1], xrecv.at[2 * j + 1])
+            arrived(rbuf.at[2 * j + 1], xrecv.at[j // 2])
             forward(2 * j + 1).start()
 
     def collect(pair):
@@ -226,7 +228,7 @@
 
             @pl.when(jnp.logical_and(slot > 0, core != (j + odd * xl) % 2))
             def _():
-                arrived(rbuf.at[slot], frecv.at[slot])
+                arrived(rbuf.at[slot], frecv.at[slot % 2 * 4 + slot // 4])
         prepare(pair)
 
     def prepare(pair):
@@ -340,72 +342,68 @@
             products(before, b, k[b])
             k[b] = kern
 
+    def arrivals(count, events):
+        for when, evens, odds, pairs in events:
+            @pl.when(count == when)
+            def _():
+                for j in evens:
+                    pass_even(j)
+                for j in odds:
+                    pass_odd(j)
+                for pair in pairs:
+                    collect(pair)
+
     def work(step, _):
-        later = step + 1
-
-        def arrivals(events):
-            for when, evens, odds, pairs in events:
-                @pl.when(later == when)
-                def _():
-                    for j in evens:
-                        pass_even(j)
-                    for j in odds:
-                        pass_odd(j)
-                    for pair in pairs:
-                        collect(pair)
-
-        @pl.when(later < 8)
-        def _():
-            arrivals(((1, (6,), (0,), (1,)), (2, (3,), (1,), (2,)), (3, (7,), (), ()), (4, (5,), (), ()), (5, (4,), (), ()),
-                      (6, (), (2,), ()), (7, (), (), (3,))))
-
-            @pl.when(later == 3)
+        arrivals(step, ((0, (6,), (0,), (1,)), (1, (3,), (1,), (2,))))
+        tiles(step)
+        return 0
+
+    def work_two(half, _):
+        @pl.when(half < 5)
+        def _():
+            arrivals(half, ((1, (7, 5), (), ()), (2, (4,), (2,), ()), (3, (), (), (3,)), (4, (), (3, 4, 5, 6, 7), ())))
+
+            @pl.when(half == 1)
             def _():
                 @pl.when(core == 1)
                 def _():
-                    arrived(cbuf.at[1], lrecv.at[1])
+                    arrived(cbuf.at[1], lrecv.at[0])
                     last_relay().start()
-                arrived(cbuf.at[2], lrecv.at[2])
+                arrived(cbuf.at[2], lrecv.at[1])
 
                 def middle(h, _):
                     column(h)
                     return 0
                 lax.fori_loop(1, 3, middle, 0)
 
-        @pl.when(later >= 8)
-        def _():
-            arrivals(((9, (), (3, 4, 5), ()), (10, (), (6, 7), (4,))))
-
-            @pl.when(later == 8)
+            @pl.when(half == 3)
             def _():
-                arrived(cbuf.at[4], lrecv.at[4])
+                arrived(cbuf.at[4], lrecv.at[2])
                 column(4)
 
-        tiles(step)
-        return 0
-
-    def work_two(half, _):
-        for when, pair in ((6, 5), (7, 6), (8, 7)):
-            @pl.when(half == when)
-            def _():
-                collect(pair)
+        @pl.when(half >= 5)
+        def _():
+            arrivals(half, ((5, (), (), (4,)), (6, (), (), (5,)), (7, (), (), (6,)), (8, (), (), (7,))))
 
         tiles(2 * half)
         tiles(2 * half + 1)
-        for when, trades, sends, chunks in ((5, (3,), (), ()), (6, (0,), (3,), (3,)), (7, (1, 2, 4), (0,), (4,)), (8, (5,), (1, 2, 4), ()),
-                                            (9, (6,), (5,), ())):
-            @pl.when(half == when)
-            def _():
-                for pair in trades:
-                    trade(pair).start()
-                for pair in sends:
-                    send_rows(pair)
-                for h in chunks:
-                    send_columns(h)
+
+        @pl.when(half >= 5)
+        def _():
+            for when, trades, sends, chunks in ((5, (3, 0), (), ()), (6, (1, 2), (3, 0), ()), (7, (4,), (1, 2), (3, 4)),
+                                                (8, (5,), (4,), ()), (9, (6,), (5,), ())):
+                @pl.when(half == when)
+                def _():
+                    for pair in trades:
+                        trade(pair).start()
+                    for pair in sends:
+                        send_rows(pair)
+                    for h in chunks:
+                        send_columns(h)
         return 0
 
-    lax.fori_loop(0, WORK // 2, work, 0)
-    lax.fori_loop(WORK // 4, WORK // 2, work_two, 0)
+    lax.fori_loop(0, 2, work, 0)
+    lax.fori_loop(1, WORK // 2, work_two, 0)
     for b in range(COLS):
         products(WORK - 1, b, k[b])
     trade(7).start()
@@ -516,9 +514,9 @@
             vmem((2, COLS, 2, PROBES, 128), F32),
             vmem((COLS, CHIP, LANES), F32),
             vmem((COLS, CHIP, LANES), BF),
-            dma, dma, dma, dma, dma((PLACES // 2,)), dma((PLACES // 2, 2)), dma((PLACES // 2,)), dma((PLACES,)),
-            dma((PLACES,)), dma((PLACES,)), dma((2, COLS)), dma((COLS, 2)), dma, dma((COLS,)),
-            dma((PLACES // 2,)), dma((PLACES // 2,)), dma((PLACES, 2)), dma((PLACES,)), dma((COLS, 2)), dma((2, COLS)), dma((2,)),
+            dma, dma, dma, dma, dma((PLACES // 2,)), dma((PLACES // 4, 2)), dma((PLACES // 4,)), dma((PLACES // 4,)),
+            dma((PLACES // 2,)), dma((PLACES // 2,)), dma((2, COLS)), dma((COLS, 2)), dma, dma((3,)),
+            dma((PLACES // 2,)), dma((PLACES // 2,)), dma((PLACES // 2, 2)), dma((PLACES,)), dma((COLS, 2)), dma((2, COLS)), dma((2,)),
         ],
         compiler_params=pltpu.CompilerParams(
             collective_id=0, has_side_effects=True, vmem_limit_bytes=40 * 1024 * 1024

time: 56.7 us -> 56 us (0.988)
  Pallas kernels: 54.5 us -> 53.7 us
    pallas_call x1, Pallas kernels: 54.5 us -> 53.7 us  [on_device(): pl.pallas_call(lambda *refs: kernel(float(total) ** (-0.5), *refs), out_s...]
where the time goes in v5:
time: 56 us; the launch traced here: 55.8 us
  Pallas kernels  53.7 us (96%)
  local copies, waits for them, and re-layouts  2.06 us (4%)
    pallas_call x1, Pallas kernels, on_device(): pl.pallas_call(lambda *refs: kernel(float(total) ** (-0.5), *refs), out_s...  53.7 us
    unnamed x5, local copies, waits for them, and re-layouts  2.06 us

profile of v5, /device:TPU:1, one launch (start us, length us, event | category | flops | bytes accessed | tf_op | source)
XLA Modules:
  0.0 55.8 jit_solution(10222471008251556101)
XLA Ops:
  0.0 0.0 copy-start
  0.0 0.8 %copy-done = bf16[64,192]{1,0:T(8,128)(2,1)S(1)} copy-done((bf16[64,192]{1,0:T(8,128)(2,1)S(1)}, bf16[64,192]{1,0:T(8,128)(2,1)}, u32[]{:S(2)}) %copy-start) | copy-done | bytes 24600
  0.8 0.0 copy-start.1
  0.8 0.7 %copy-done.1 = bf16[16,192]{1,0:T(8,128)(2,1)S(1)} copy-done((bf16[16,192]{1,0:T(8,128)(2,1)S(1)}, bf16[16,192]{1,0:T(8,128)(2,1)}, u32[]{:S(2)}) %copy-start.1) | copy-done | bytes 6168
  1.5 53.7 %matern_product.1 = f32[16,192]{1,0:T(8,128)S(1)} custom-call(bf16[64,192]{1,0:T(8,128)(2,1)S(1)} %copy-done, bf16[16,192]{1,0:T(8,128)(2,1)S(1)} %copy-done.1), custom_call_target="tpu_custom_call" | custom-call | tf_op jit(solution)/shard_map/matern_product/pallas_call | solution.py:495
  55.2 0.6 %copy.4 = f32[16,192]{1,0:T(8,128)} copy(f32[16,192]{1,0:T(8,128)S(1)} %matern_product.1) | data formatting | bytes 24576
Async XLA Ops:
  0.0 0.8 %copy-start = (bf16[64,192]{1,0:T(8,128)(2,1)S(1)}, bf16[64,192]{1,0:T(8,128)(2,1)}, u32[]{:S(2)}) copy-start(bf16[64,192]{1,0:T(8,128)(2,1)} %refs_0_.1) | copy-start | bytes 73732
  0.8 0.7 %copy-start.1 = (bf16[16,192]{1,0:T(8,128)(2,1)S(1)}, bf16[16,192]{1,0:T(8,128)(2,1)}, u32[]{:S(2)}) copy-start(bf16[16,192]{1,0:T(8,128)(2,1)} %refs_1_.1) | copy-start | bytes 18436

commit v6 on v5

--- a/solution.py
+++ b/solution.py
@@ -99,8 +99,12 @@
     @pl.loop(1, 16)
     def _(step):
         for c in range(2):
+            pl.semaphore_signal(barrier, inc=1, device_id=device((xh + step // 8) % 2, (z + step) % 8, place, c), device_id_type=MESH)
+
+    @pl.loop(1, 16)
+    def _(step):
+        for c in range(2):
             pl.semaphore_signal(barrier, inc=1, device_id=device(xh, z, (place + step) % PLACES, c), device_id_type=MESH)
-            pl.semaphore_signal(barrier, inc=1, device_id=device((xh + step // 8) % 2, (z + step) % 8, place, c), device_id_type=MESH)
 
     copies = [pltpu.make_async_copy(points, pts, isem.at[0]), pltpu.make_async_copy(probes, prb, isem.at[1])]
     for copy in copies:
@@ -310,26 +314,18 @@
         across(0).start()
         cbuf[3] = rbuf[0]
 
+    pass_even(1)
+
     @pl.when(core == 1)
     def _():
         halves(3)
         for taker, h in RELAYED:
             relay(taker, h).start()
 
-    pass_even(1)
-
-    @pl.when(core == 0)
-    def _():
-        halves(1)
-        last_relay().start()
+    column(3)
     collect(0)
     halves(0)
-
-    def first(i, _):
-        column(3 * i)
-        return 0
-
-    lax.fori_loop(0, 2, first, 0)
+    column(0)
     pass_even(2)
     for b in range(COLS):
         cross(0, b)
@@ -365,10 +361,14 @@
 
             @pl.when(half == 1)
             def _():
+                @pl.when(core == 0)
+                def _():
+                    halves(1)
+
                 @pl.when(core == 1)
                 def _():
                     arrived(cbuf.at[1], lrecv.at[0])
-                    last_relay().start()
+                last_relay().start()
                 arrived(cbuf.at[2], lrecv.at[1])
 
                 def middle(h, _):
@@ -407,9 +407,9 @@
     for b in range(COLS):
         products(WORK - 1, b, k[b])
     trade(7).start()
+    send_rows(6)
     for h in (2, 1, 0):
         send_columns(h)
-    send_rows(6)
     send_rows(7)
 
     share().wait_send()

time: 56 us -> 55.8 us (level)
  no operation moved by 1% of the time
where the time goes in v6:
time: 55.8 us; the launch traced here: 55.6 us
  Pallas kernels  53.5 us (96%)
  local copies, waits for them, and re-layouts  2.06 us (4%)
    pallas_call x1, Pallas kernels, on_device(): pl.pallas_call(lambda *refs: kernel(float(total) ** (-0.5), *refs), out_s...  53.5 us
    unnamed x5, local copies, waits for them, and re-layouts  2.06 us

profile of v6, /device:TPU:1, one launch (start us, length us, event | category | flops | bytes accessed | tf_op | source)
XLA Modules:
  0.0 55.6 jit_solution(15882075097706100625)
XLA Ops:
  0.0 0.0 copy-start
  0.0 0.8 %copy-done = bf16[64,192]{1,0:T(8,128)(2,1)S(1)} copy-done((bf16[64,192]{1,0:T(8,128)(2,1)S(1)}, bf16[64,192]{1,0:T(8,128)(2,1)}, u32[]{:S(2)}) %copy-start) | copy-done | bytes 24600
  0.8 0.0 copy-start.1
  0.8 0.7 %copy-done.1 = bf16[16,192]{1,0:T(8,128)(2,1)S(1)} copy-done((bf16[16,192]{1,0:T(8,128)(2,1)S(1)}, bf16[16,192]{1,0:T(8,128)(2,1)}, u32[]{:S(2)}) %copy-start.1) | copy-done | bytes 6168
  1.5 53.5 %matern_product.1 = f32[16,192]{1,0:T(8,128)S(1)} custom-call(bf16[64,192]{1,0:T(8,128)(2,1)S(1)} %copy-done, bf16[16,192]{1,0:T(8,128)(2,1)S(1)} %copy-done.1), custom_call_target="tpu_custom_call" | custom-call | tf_op jit(solution)/shard_map/matern_product/pallas_call | solution.py:495
  55.0 0.6 %copy.4 = f32[16,192]{1,0:T(8,128)} copy(f32[16,192]{1,0:T(8,128)S(1)} %matern_product.1) | data formatting | bytes 24576
Async XLA Ops:
  0.0 0.8 %copy-start = (bf16[64,192]{1,0:T(8,128)(2,1)S(1)}, bf16[64,192]{1,0:T(8,128)(2,1)}, u32[]{:S(2)}) copy-start(bf16[64,192]{1,0:T(8,128)(2,1)} %refs_0_.1) | copy-start | bytes 73732
  0.8 0.7 %copy-start.1 = (bf16[16,192]{1,0:T(8,128)(2,1)S(1)}, bf16[16,192]{1,0:T(8,128)(2,1)}, u32[]{:S(2)}) copy-start(bf16[16,192]{1,0:T(8,128)(2,1)} %refs_1_.1) | copy-start | bytes 18436

commit v7 on v6

--- a/solution.py
+++ b/solution.py
@@ -519,7 +519,7 @@
             dma((PLACES // 2,)), dma((PLACES // 2,)), dma((PLACES // 2, 2)), dma((PLACES,)), dma((COLS, 2)), dma((2, COLS)), dma((2,)),
         ],
         compiler_params=pltpu.CompilerParams(
-            collective_id=0, has_side_effects=True, vmem_limit_bytes=40 * 1024 * 1024
+            collective_id=0, has_side_effects=True, vmem_limit_bytes=60 * 1024 * 1024
         ),
         name="matern_product",
     )(points, probes)

time: 55.8 us -> 55.8 us (level)
  local copies, waits for them, and re-layouts: 2.06 us -> 1.32 us
  Pallas kernels: 53.5 us -> 54.2 us
    unnamed x5 -> x1, local copies, waits for them, and re-layouts: 2.06 us -> 1.32 us
    pallas_call x1, Pallas kernels: 53.5 us -> 54.2 us  [on_device(): pl.pallas_call(lambda *refs: kernel(float(total) ** (-0.5), *refs), out_s...]
where the time goes in v7:
time: 55.8 us; the launch traced here: 55.5 us
  Pallas kernels  54.2 us (97%)
  local copies, waits for them, and re-layouts  1.32 us (2%)
    pallas_call x1, Pallas kernels, on_device(): pl.pallas_call(lambda *refs: kernel(float(total) ** (-0.5), *refs), out_s...  54.2 us
    unnamed x1, local copies, waits for them, and re-layouts  1.32 us

profile of v7, /device:TPU:1, one launch (start us, length us, event | category | flops | bytes accessed | tf_op | source)
XLA Modules:
  0.0 55.5 jit_solution(11211143385906080159)
XLA Ops:
  0.0 54.2 %matern_product.1 = f32[16,192]{1,0:T(8,128)} custom-call(bf16[64,192]{1,0:T(8,128)(2,1)} %refs_0_.1, bf16[16,192]{1,0:T(8,128)(2,1)} %refs_1_.1), custom_call_target="tpu_custom_call" | custom-call | tf_op jit(solution)/shard_map/matern_product/pallas_call | solution.py:495
  54.2 1.3 %copy.4 = f32[16,192]{1,0:T(8,128)} copy(f32[16,192]{1,0:T(8,128)} %matern_product.1) | data formatting | bytes 24576
